TPU v7x, 32 devices: a whole 2x2x4 slice. The times are simulated.
32 devices in a mesh: lon: 8 (over z, core), lat: 4 (over y, x).
Axes of the slice: x: 2, y: 2, z: 4, core: 2. Of those that a mesh axis runs over, the one named last changes fastest.
Arguments:
- tokens: bfloat16 [2, 48, 96, 192], P(None, 'lat', 'lon'), may hold values from -6 to 6
- cotangent: bfloat16 [2, 48, 96, 192], P(None, 'lat', 'lon'), may hold values from -6 to 6
- qkv_codes: int32 [192, 576], replicated, may hold values from -128 to 127
- proj_codes: int32 [192, 192], replicated, may hold values from -128 to 127
- up_codes: int32 [192, 768], replicated, may hold values from -128 to 127
- down_codes: int32 [768, 192], replicated, may hold values from -128 to 127
- bit_widths: int32 [4], replicated, may hold values from 6 to 8
- quant_scales: int32 [4], replicated, may hold values from 300 to 599
- bias_table: bfloat16 [8, 1, 6, 3312], P('lat'), may hold values from -4 to 302
- bias_index: int32 [20736], replicated, may hold values from 0 to 3311
- merge_weight: bfloat16 [768, 384], replicated, may hold values from -0.21875 to 0.21875
Outputs:
- merged: bfloat16 [2, 24, 48, 384], P(None, 'lat', 'lon')
- grad_tokens: bfloat16 [2, 48, 96, 192], P(None, 'lat', 'lon')
- grad_qkv: bfloat16 [192, 576], replicated
- grad_proj: bfloat16 [192, 192], replicated
- grad_up: bfloat16 [192, 768], replicated
- grad_down: bfloat16 [768, 192], replicated
All inputs are finite; a program needn't handle non-finite values.
Results may differ from a plain program's by a relative error of at most 0.024.
The roundings to bfloat16 on the way count: a program that leaves them out, or rounds other values in their place, can miss the bound.
Values may be sent and summed in bfloat16 or wider, within the bound.
A program may use at most 128 MiB of HBM per device.

v0:
```python
import math

import jax
import jax.numpy as jnp
from jax import lax
from jax.sharding import PartitionSpec as P

C = 192
HEADS = 6
FF = 768
HEAD_DIM = 32
WLEV = 2
WLAT = 6
WLON = 12
LAT_PAD = 11
WTOK = 144


EPSILON = 1e-05
MASKED = -1000000000.0


def from_behind(x, axis, by):
    count = lax.axis_size(axis)
    pairs = [(i, i + by) for i in range(count) if 0 <= i + by < count]
    return lax.ppermute(x, axis, pairs)


def passed_along(block, axis, distance):
    devices = range(lax.axis_size(axis))
    route = [((i - distance) % len(devices), i) for i in devices]
    return lax.ppermute(block, axis, route)


def product(left, right):
    return jnp.dot(left, right, preferred_element_type=jnp.float32)


def crossed(left, right):
    return jnp.dot(left.T, right, preferred_element_type=jnp.float32)


def dequant(int_codes, bit_count, quant_scale, fan_in):
    largest = jnp.left_shift(jnp.ones((), jnp.int32), bit_count - 1) - 1
    clipped = jnp.clip(int_codes, -largest, largest).astype(jnp.float32)
    factor = math.sqrt(C / fan_in) / quant_scale.astype(jnp.float32)
    return (clipped * factor).astype(jnp.bfloat16)


def normalize(values):
    center = values - jnp.mean(values, axis=-1, keepdims=True)
    spread = jnp.mean(center * center, axis=-1, keepdims=True)
    return center * lax.rsqrt(spread + EPSILON)


def norm_back(source, upstream):
    pullback = jax.vjp(normalize, source.astype(jnp.float32))[1]
    return pullback(upstream.astype(jnp.float32))[0]


def gelu_back(pre_act, upstream):
    pullback = jax.vjp(jax.nn.gelu, pre_act)[1]
    return pullback(upstream.astype(jnp.float32))[0]


def allowed_table(lat_start, lat_limit, level_count, row_windows):
    position = jnp.arange(WTOK, dtype=jnp.int32)
    level_in = position // (WLAT * WLON)
    row_in = position // WLON % WLAT
    window_level = WLEV * jnp.arange(level_count // WLEV, dtype=jnp.int32)
    levels = (window_level[:, None] + level_in[None, :] + 1) % level_count
    group = (levels + 1) // 2
    same = group[:, :, None] == group[:, None, :]
    lat_rows = (
        lat_start + WLAT * jnp.arange(row_windows, dtype=jnp.int32)[:, None] + row_in[None, :]
    )
    key_ok = (lat_rows >= 0) & (lat_rows < lat_limit)
    allowed = same[:, None, :, :] & key_ok[None, :, None, :]
    return allowed.reshape(-1, WTOK, WTOK)


def window_terms(table_rows, bias_index, lat_start, lat_limit, level_count):
    row_windows = table_rows.shape[0]
    level_windows = level_count // WLEV
    gathered = table_rows[:, :, :, bias_index].astype(jnp.float32)
    gathered = gathered.reshape(row_windows, level_windows, HEADS, WTOK, WTOK).transpose(
        1, 0, 2, 3, 4
    )
    gathered = gathered.reshape(level_windows * row_windows, HEADS, WTOK, WTOK)
    return (gathered, allowed_table(lat_start, lat_limit, level_count, row_windows))


def to_windows(window_frame):
    level_count, row_count, col_count, feat_count = window_frame.shape
    rolled = jnp.roll(window_frame, -1, axis=0)
    pieces = rolled.reshape(
        level_count // WLEV, WLEV, row_count // WLAT, WLAT, col_count // WLON, WLON, feat_count
    )
    return pieces.transpose(0, 2, 4, 1, 3, 5, 6).reshape(-1, WTOK, feat_count)


def from_windows(windows, level_count, row_count, col_count):
    feat_count = windows.shape[-1]
    pieces = windows.reshape(
        level_count // WLEV, row_count // WLAT, col_count // WLON, WLEV, WLAT, WLON, feat_count
    )
    pieces = pieces.transpose(0, 3, 1, 4, 2, 5, 6).reshape(
        level_count, row_count, col_count, feat_count
    )
    return jnp.roll(pieces, 1, axis=0)


def attend(windows, bias_terms, allowed):
    window_count = windows.shape[0]
    group_count = bias_terms.shape[0]
    query_part, key_part, value_part = jnp.split(windows.astype(jnp.float32), 3, axis=-1)
    query_part = query_part.reshape(window_count, WTOK, HEADS, HEAD_DIM)
    key_part = key_part.reshape(window_count, WTOK, HEADS, HEAD_DIM)
    value_part = value_part.reshape(window_count, WTOK, HEADS, HEAD_DIM)
    scores = jnp.einsum("wqhd,wkhd->whqk", query_part, key_part) * HEAD_DIM ** (-0.5)
    scores = (
        scores.reshape(group_count, window_count // group_count, HEADS, WTOK, WTOK)
        + bias_terms[:, None]
    )
    scores = jnp.where(allowed[:, None, None], scores, MASKED)
    top_score = jnp.max(scores, axis=-1, keepdims=True)
    weights = jnp.exp(scores - top_score)
    weights = (weights / jnp.sum(weights, axis=-1, keepdims=True)).astype(jnp.bfloat16)
    weights = weights.reshape(window_count, HEADS, WTOK, WTOK)
    mixed = jnp.einsum("whqk,wkhd->wqhd", weights.astype(jnp.float32), value_part)
    return mixed.reshape(window_count, WTOK, C)


def merge_patches(final, merge_weight):
    level_count, row_count, col_count, feat_count = final.shape
    grouped = final.reshape(level_count, row_count // 2, 2, col_count // 2, 2, feat_count)
    grouped = grouped.transpose(0, 1, 3, 2, 4, 5).reshape(-1, 4 * feat_count)
    normed = normalize(grouped.astype(jnp.float32)).astype(jnp.bfloat16)
    merged = product(normed, merge_weight).astype(jnp.bfloat16)
    return merged.reshape(level_count, row_count // 2, col_count // 2, 2 * feat_count)


def pull_rim(source):
    lat_part = from_behind(source[:, -(WLAT // 2) :], "lat", 1)
    upper = jnp.concatenate([lat_part, source[:, : -(WLAT // 2)]], axis=1)
    lon_part = passed_along(upper[:, :, -(WLON // 2) :], "lon", 1)
    return jnp.concatenate([lon_part, upper[:, :, : -(WLON // 2)]], axis=2)


def push_rim(window_frame):
    lon_part = passed_along(window_frame[:, :, : WLON // 2], "lon", -1)
    upper = jnp.concatenate([window_frame[:, :, WLON // 2 :], lon_part], axis=2)
    lat_part = from_behind(upper[:, : WLAT // 2], "lat", -1)
    return jnp.concatenate([upper[:, WLAT // 2 :], lat_part], axis=1)


def after_attention(start_flat, heads_flat, d_out, w_proj, w_up, w_down):
    resid = (start_flat.astype(jnp.float32) + product(heads_flat, w_proj)).astype(jnp.bfloat16)
    normed_two = normalize(resid.astype(jnp.float32)).astype(jnp.bfloat16)
    pre_act = product(normed_two, w_up)
    hidden = jax.nn.gelu(pre_act).astype(jnp.bfloat16)
    final = resid.astype(jnp.float32) + product(hidden, w_down)
    down_total = crossed(hidden, d_out)
    d_hidden = product(d_out, w_down.T).astype(jnp.bfloat16)
    d_pre = gelu_back(pre_act, d_hidden).astype(jnp.bfloat16)
    up_total = crossed(normed_two, d_pre)
    d_normed_two = product(d_pre, w_up.T).astype(jnp.bfloat16)
    d_resid = (d_out.astype(jnp.float32) + norm_back(resid, d_normed_two)).astype(jnp.bfloat16)
    proj_total = crossed(heads_flat, d_resid)
    d_heads = product(d_resid, w_proj.T).astype(jnp.bfloat16)
    return (final, d_resid, d_heads, proj_total, up_total, down_total)


def per_device(
    tokens,
    cotangent,
    qkv_codes,
    proj_codes,
    up_codes,
    down_codes,
    bit_widths,
    quant_scales,
    bias_table,
    bias_index,
    merge_weight,
):
    level_count, row_count, col_count, feat_count = tokens.shape
    token_count = level_count * row_count * col_count
    grid_shape = (level_count, row_count, col_count)
    lat_limit = lax.axis_size("lat") * row_count - LAT_PAD
    lat_index = lax.axis_index("lat")
    lat_start = lat_index * row_count - WLAT // 2
    w_qkv = dequant(qkv_codes, bit_widths[0], quant_scales[0], C)
    w_proj = dequant(proj_codes, bit_widths[1], quant_scales[1], C)
    w_up = dequant(up_codes, bit_widths[2], quant_scales[2], C)
    w_down = dequant(down_codes, bit_widths[3], quant_scales[3], FF)
    bias_terms, allowed = window_terms(bias_table, bias_index, lat_start, lat_limit, level_count)

    def local_attend(windows):
        return attend(windows, bias_terms, allowed)

    row_ids = lat_index * row_count + jnp.arange(row_count, dtype=jnp.int32)
    row_mask = (row_ids < lat_limit)[None, :, None, None]
    start = jnp.where(row_mask, tokens, jnp.zeros_like(tokens))
    start_flat = start.reshape(token_count, feat_count)
    normed = normalize(start.astype(jnp.float32)).astype(jnp.bfloat16)
    own_qkv = (
        product(normed.reshape(token_count, feat_count), w_qkv)
        .astype(jnp.bfloat16)
        .reshape(grid_shape + (3 * feat_count,))
    )
    frame_qkv = pull_rim(own_qkv)
    heads_windows, pullback = jax.vjp(local_attend, to_windows(frame_qkv))
    heads_out = push_rim(
        from_windows(heads_windows.astype(jnp.bfloat16), level_count, row_count, col_count)
    )
    heads_flat = heads_out.reshape(token_count, feat_count)
    d_out = jnp.where(row_mask, cotangent, jnp.zeros_like(cotangent)).reshape(
        token_count, feat_count
    )
    final, d_resid, d_heads, proj_total, up_total, down_total = after_attention(
        start_flat, heads_flat, d_out, w_proj, w_up, w_down
    )
    frame_grad = pull_rim(d_heads.reshape(grid_shape + (feat_count,)))
    d_frame = from_windows(
        pullback(to_windows(frame_grad).astype(jnp.float32))[0], level_count, row_count, col_count
    )
    d_qkv = push_rim(d_frame).reshape(token_count, 3 * feat_count)
    qkv_total = crossed(normed.reshape(token_count, feat_count), d_qkv)
    d_normed = product(d_qkv, w_qkv.T).astype(jnp.bfloat16)
    grad_flat = d_resid.astype(jnp.float32) + norm_back(start_flat, d_normed)
    grad_tokens = jnp.where(row_mask, grad_flat.reshape(grid_shape + (feat_count,)), 0.0).astype(
        jnp.bfloat16
    )
    final_owned = jnp.where(row_mask, final.reshape(grid_shape + (feat_count,)), 0.0).astype(
        jnp.bfloat16
    )
    merged = merge_patches(final_owned, merge_weight)
    summed = lax.psum((qkv_total, proj_total, up_total, down_total), ("lon", "lat"))
    return (
        merged,
        grad_tokens,
        summed[0].astype(jnp.bfloat16),
        summed[1].astype(jnp.bfloat16),
        summed[2].astype(jnp.bfloat16),
        summed[3].astype(jnp.bfloat16),
    )


def solution(mesh):
    placed = (
        P(None, "lat", "lon", None),
        P(None, "lat", "lon", None),
        P(),
        P(),
        P(),
        P(),
        P(),
        P(),
        P("lat", None, None, None),
        P(),
        P(),
    )
    return jax.shard_map(
        per_device,
        mesh=mesh,
        in_specs=placed,
        out_specs=(P(None, "lat", "lon", None), P(None, "lat", "lon", None), P(), P(), P(), P()),
        check_vma=False,
    )
```

profile of v0, /device:TPU:1, one launch (start us, length us, event | category | flops | bytes accessed | tf_op | source)
XLA Modules:
  0.0 278.0 jit_solution(9402266574560985977)
XLA Ops:
  10.0 3.9 %collective-permute-start = (bf16[2,3,12,576]{3,2,1,0:T(8,128)(2,1)S(1)}, bf16[2,3,12,576]{3,2,1,0:T(8,128)(2,1)S(1)}, u32[]{:S(2)}, u32[]{:S(2)}) collective-permute-start(bf16[2,3,12,576]{3,2,1,0:T(8,128)(2,1)S(1)} %slice.154), channel_id=1, source_target_pairs={{0,1},{1,2},{2,3},{4,5},{5,6},{6,7},{8,9},{9,10},{10,11},{12,13},{... | collective-permute-start | bytes 248840 | tf_op jit(solution)/shard_map/ppermute | solution.py:26
  16.6 2.8 %collective-permute-start.1 = (bf16[2,12,6,576]{3,2,1,0:T(8,128)(2,1)}, bf16[2,12,6,576]{3,2,1,0:T(8,128)(2,1)}, u32[]{:S(2)}, u32[]{:S(2)}) collective-permute-start(bf16[2,12,6,576]{3,2,1,0:T(8,128)(2,1)} %fusion.33), channel_id=1, source_target_pairs={{28,0},{0,4},{4,8},{8,12},{12,16},{16,20},{20,24},{24,28},{29,1},{... | collective-permute-start | bytes 497672 | tf_op jit(solution)/shard_map/ppermute | solution.py:32
  20.9 3.6 %copy.35 = bf16[2,1,6,3312]{2,0,3,1:T(2,128)(2,1)S(1)} copy(bf16[2,1,6,3312]{3,0,2,1:T(2,128)(2,1)} %param.19) | data formatting | bytes 158976 | tf_op args[8]
  24.5 51.2 %gather_fusion = bf16[20736,2,6]{2,1,0:T(2,128)(2,1)} fusion(bf16[2,6,3312]{1,0,2:T(2,128)(2,1)S(1)} %bitcast.85, s32[21504]{0:T(1024)S(1)} %copy-done.24), kind=kCustom, calls=%fused_computation | custom fusion | bytes 1078272 | tf_op jit(solution)/shard_map/gather | solution.py:85
  75.7 11.4 %convert_element_type.254 = f32[20736,2,6]{2,1,0:T(2,128)} convert(bf16[20736,2,6]{2,1,0:T(2,128)(2,1)} %gather_fusion) | non-fusion elementwise | flops 248832 | bytes 1492992 | tf_op jit(solution)/shard_map/convert_element_type | solution.py:85
  87.2 31.1 %copy.37 = f32[2,6,144,144]{2,3,1,0:T(8,128)} copy(f32[2,6,144,144]{1,0,3,2:T(2,128)} %bitcast.84) | data formatting | bytes 1990656 | tf_op jit(solution)/shard_map/convert_element_type | solution.py:85
  127.1 2.1 fusion.71
  130.1 2.0 convert_reduce_fusion
  132.1 1.7 copy.32
  133.9 1.9 fusion.9
  135.7 2.2 copy.39
  137.9 2.2 convert_element_type.208
  142.6 2.7 collective-permute-done.2
  146.9 4.0 %collective-permute-done.3 = bf16[2,3,12,192]{3,2,1,0:T(8,128)(2,1)S(1)} collective-permute-done((bf16[2,3,12,192]{3,2,1,0:T(8,128)(2,1)S(1)}, bf16[2,3,12,192]{3,2,1,0:T(8,128)(2,1)S(1)}, u32[]{:S(2)}, u32[]{:S(2)}) %collective-permute-start.3) | collective-permute-done | bytes 27680 | tf_op jit(solution)/shard_map/ppermute | solution.py:26
  151.7 1.6 reshape.592
  166.9 4.9 %collective-permute-start.4 = (bf16[2,3,12,192]{3,2,1,0:T(8,128)(2,1)}, bf16[2,3,12,192]{3,2,1,0:T(8,128)(2,1)}, u32[]{:S(2)}, u32[]{:S(2)}) collective-permute-start(bf16[2,3,12,192]{3,2,1,0:T(8,128)(2,1)} %slice.166), channel_id=1, source_target_pairs={{0,1},{1,2},{2,3},{4,5},{5,6},{6,7},{8,9},{9,10},{10,11},{12,13},{... | collective-permute-start | bytes 82952 | tf_op jit(solution)/shard_map/ppermute | solution.py:26
  171.7 1.7 reshape.593
  183.8 1.9 reshape.603
  187.7 2.1 reshape.598
  189.8 2.1 copy.45
  191.9 1.6 fusion.3
  203.2 3.1 %collective-permute-done.6 = bf16[2,12,6,576]{3,2,1,0:T(8,128)(2,1)S(1)} collective-permute-done((bf16[2,12,6,576]{3,2,1,0:T(8,128)(2,1)S(1)}, bf16[2,12,6,576]{3,2,1,0:T(8,128)(2,1)S(1)}, u32[]{:S(2)}, u32[]{:S(2)}) %collective-permute-start.6) | collective-permute-done | bytes 165920 | tf_op jit(solution)/shard_map/ppermute | solution.py:32
  207.8 4.2 %collective-permute-done.7 = bf16[2,3,12,576]{3,2,1,0:T(8,128)(2,1)S(1)} collective-permute-done((bf16[2,3,12,576]{3,2,1,0:T(8,128)(2,1)S(1)}, bf16[2,3,12,576]{3,2,1,0:T(8,128)(2,1)S(1)}, u32[]{:S(2)}, u32[]{:S(2)}) %collective-permute-start.7) | collective-permute-done | bytes 82976 | tf_op jit(solution)/shard_map/ppermute | solution.py:26
  216.3 61.7 %all-reduce.2 = (bf16[192,576]{1,0:T(8,128)(2,1)}, bf16[192,192]{1,0:T(8,128)(2,1)}, bf16[192,768]{1,0:T(8,128)(2,1)}, bf16[768,192]{0,1:T(8,128)(2,1)}) all-reduce(f32[192,576]{1,0:T(8,128)S(1)} %copy-done.20, f32[192,192]{1,0:T(8,128)S(1)} %copy-done.16, ...), channel_id=1, replica_groups=mesh['lon'=8,'lat'=4] {'lon','lat'}, use_global_device_ids=true, to_apply=%region_15.16 | all-reduce | flops 442368 | bytes 2654208 | tf_op jit(solution)/shard_map/psum | solution.py:239
  (205 shorter events, 63.4 us)
Async XLA Ops:
  0.6 201.6 %copy-start = (bf16[768,384]{1,0:T(8,128)(2,1)S(1)}, bf16[768,384]{1,0:T(8,128)(2,1)}, u32[]{:S(2)}) copy-start(bf16[768,384]{1,0:T(8,128)(2,1)} %param.21) | copy-start | bytes 1769476
  0.6 13.5 %copy-start.32 = (s32[20736]{0:T(1024)S(1)}, s32[20736]{0:T(1024)}, u32[]{:S(2)}) copy-start(s32[20736]{0:T(1024)} %param.20) | copy-start | bytes 248836
  0.7 14.1 %copy-start.38 = (pred[12]{0:T(512)(128)(4,1)}, pred[12]{0:T(512)(128)(4,1)S(1)}, u32[]{:S(2)}) copy-start(pred[12]{0:T(512)(128)(4,1)S(1)} %add_compare_fusion.1) | copy-start | bytes 40
  1.9 12.9 %copy-start.3 = (bf16[2,12,12,192]{3,0,2,1:T(2,128)(2,1)S(1)}, bf16[2,12,12,192]{3,0,2,1:T(2,128)(2,1)}, u32[]{:S(2)}) copy-start(bf16[2,12,12,192]{3,0,2,1:T(2,128)(2,1)} %param.11) | copy-start | bytes 331780
  1.9 12.9 %copy-start.31 = (bf16[2,12,12,192]{3,0,2,1:T(2,128)(2,1)S(1)}, bf16[2,12,12,192]{3,0,2,1:T(2,128)(2,1)}, u32[]{:S(2)}) copy-start(bf16[2,12,12,192]{3,0,2,1:T(2,128)(2,1)} %param.12) | copy-start | bytes 331780
  1.9 18.3 %copy-start.29 = (f32[2,12,12]{2,1,0:T(8,128)}, f32[2,12,12]{2,1,0:T(8,128)S(1)}, u32[]{:S(2)}) copy-start(f32[2,12,12]{2,1,0:T(8,128)S(1)} %broadcast_multiply_fusion) | copy-start | bytes 3460
  3.2 10.8 %copy-start.35 = (f32[2,12,12]{2,1,0:T(8,128)}, f32[2,12,12]{2,1,0:T(8,128)S(1)}, u32[]{:S(2)}) copy-start(f32[2,12,12]{2,1,0:T(8,128)S(1)} %get-tuple-element.49) | copy-start | bytes 3460
  10.0 5.8 %collective-permute-start = (bf16[2,3,12,576]{3,2,1,0:T(8,128)(2,1)S(1)}, bf16[2,3,12,576]{3,2,1,0:T(8,128)(2,1)S(1)}, u32[]{:S(2)}, u32[]{:S(2)}) collective-permute-start(bf16[2,3,12,576]{3,2,1,0:T(8,128)(2,1)S(1)} %slice.154), channel_id=1, source_target_pairs={{0,1},{1,2},{2,3},{4,5},{5,6},{6,7},{8,9},{9,10},{10,11},{12,13},{... | collective-permute-start | bytes 248840 | tf_op jit(solution)/shard_map/ppermute | solution.py:26
  14.9 9.6 %copy-start.24 = (s32[21504]{0:T(1024)S(1)}, s32[21504]{0:T(1024)}, u32[]{:S(2)}) copy-start(s32[21504]{0:T(1024)} %pad_clamp_fusion) | copy-start | bytes 258052
  15.8 59.9 %copy-start.21 = (bf16[2,3,12,576]{3,2,1,0:T(8,128)(2,1)}, bf16[2,3,12,576]{3,2,1,0:T(8,128)(2,1)S(1)}, u32[]{:S(2)}) copy-start(bf16[2,3,12,576]{3,2,1,0:T(8,128)(2,1)S(1)} %collective-permute-done) | copy-start | bytes 248836
  16.6 107.4 %collective-permute-start.1 = (bf16[2,12,6,576]{3,2,1,0:T(8,128)(2,1)}, bf16[2,12,6,576]{3,2,1,0:T(8,128)(2,1)}, u32[]{:S(2)}, u32[]{:S(2)}) collective-permute-start(bf16[2,12,6,576]{3,2,1,0:T(8,128)(2,1)} %fusion.33), channel_id=1, source_target_pairs={{28,0},{0,4},{4,8},{8,12},{12,16},{16,20},{20,24},{24,28},{29,1},{... | collective-permute-start | bytes 497672 | tf_op jit(solution)/shard_map/ppermute | solution.py:32
  87.2 36.9 %copy-start.22 = (bf16[2,3,12,576]{3,2,1,0:T(8,128)(2,1)S(1)}, bf16[2,3,12,576]{3,2,1,0:T(8,128)(2,1)}, u32[]{:S(2)}) copy-start(bf16[2,3,12,576]{3,2,1,0:T(8,128)(2,1)} %copy-done.21) | copy-start | bytes 248836
  141.2 4.1 %collective-permute-start.2 = (bf16[2,12,6,192]{3,2,1,0:T(8,128)(2,1)S(1)}, bf16[2,12,6,192]{3,2,1,0:T(8,128)(2,1)S(1)}, u32[]{:S(2)}, u32[]{:S(2)}) collective-permute-start(bf16[2,12,6,192]{3,2,1,0:T(8,128)(2,1)S(1)} %get-tuple-element.45), channel_id=1, source_target_pairs={{4,0},{8,4},{12,8},{16,12},{20,16},{24,20},{28,24},{0,28},{5,1},{9... | collective-permute-start | bytes 165896 | tf_op jit(solution)/shard_map/ppermute | solution.py:32
  145.4 5.6 %collective-permute-start.3 = (bf16[2,3,12,192]{3,2,1,0:T(8,128)(2,1)S(1)}, bf16[2,3,12,192]{3,2,1,0:T(8,128)(2,1)S(1)}, u32[]{:S(2)}, u32[]{:S(2)}) collective-permute-start(bf16[2,3,12,192]{3,2,1,0:T(8,128)(2,1)S(1)} %pad_maximum_fusion.9), channel_id=1, source_target_pairs={{1,0},{2,1},{3,2},{5,4},{6,5},{7,6},{9,8},{10,9},{11,10},{13,12},{... | collective-permute-start | bytes 82952 | tf_op jit(solution)/shard_map/ppermute | solution.py:26
  153.3 3.1 %copy-start.43 = (s32[768,192]{0,1:T(8,128)S(1)}, s32[768,192]{0,1:T(8,128)}, u32[]{:S(2)}) copy-start(s32[768,192]{0,1:T(8,128)} %param.16) | copy-start | bytes 1769476
  166.9 10.1 %collective-permute-start.4 = (bf16[2,3,12,192]{3,2,1,0:T(8,128)(2,1)}, bf16[2,3,12,192]{3,2,1,0:T(8,128)(2,1)}, u32[]{:S(2)}, u32[]{:S(2)}) collective-permute-start(bf16[2,3,12,192]{3,2,1,0:T(8,128)(2,1)} %slice.166), channel_id=1, source_target_pairs={{0,1},{1,2},{2,3},{4,5},{5,6},{6,7},{8,9},{9,10},{10,11},{12,13},{... | collective-permute-start | bytes 82952 | tf_op jit(solution)/shard_map/ppermute | solution.py:26
  174.7 4.4 %copy-start.33 = (f32[2,6,6]{2,1,0:T(8,128)}, f32[2,6,6]{2,1,0:T(8,128)S(1)}, u32[]{:S(2)}) copy-start(f32[2,6,6]{2,1,0:T(8,128)S(1)} %broadcast_multiply_fusion.1) | copy-start | bytes 868
  179.1 6.6 %collective-permute-start.5 = (bf16[2,12,6,192]{3,2,1,0:T(8,128)(2,1)}, bf16[2,12,6,192]{3,2,1,0:T(8,128)(2,1)}, u32[]{:S(2)}, u32[]{:S(2)}) collective-permute-start(bf16[2,12,6,192]{3,2,1,0:T(8,128)(2,1)} %fusion.41), channel_id=1, source_target_pairs={{28,0},{0,4},{4,8},{8,12},{12,16},{16,20},{20,24},{24,28},{29,1},{... | collective-permute-start | bytes 165896 | tf_op jit(solution)/shard_map/ppermute | solution.py:32
  200.5 11.5 %copy-start.4 = (bf16[2,12,12,192]{3,0,2,1:T(2,128)(2,1)S(1)}, bf16[2,12,12,192]{3,0,2,1:T(2,128)(2,1)}, u32[]{:S(2)}) copy-start(bf16[2,12,12,192]{3,0,2,1:T(2,128)(2,1)} %param.11) | copy-start | bytes 331780
  200.5 11.5 %copy-start.30 = (f32[2,12,12]{2,1,0:T(8,128)S(1)}, f32[2,12,12]{2,1,0:T(8,128)}, u32[]{:S(2)}) copy-start(f32[2,12,12]{2,1,0:T(8,128)} %copy-done.29) | copy-start | bytes 3460
  200.5 11.5 %copy-start.36 = (f32[2,12,12]{2,1,0:T(8,128)S(1)}, f32[2,12,12]{2,1,0:T(8,128)}, u32[]{:S(2)}) copy-start(f32[2,12,12]{2,1,0:T(8,128)} %copy-done.35) | copy-start | bytes 3460
  200.5 11.5 %copy-start.39 = (pred[12]{0:T(512)(128)(4,1)S(1)}, pred[12]{0:T(512)(128)(4,1)}, u32[]{:S(2)}) copy-start(pred[12]{0:T(512)(128)(4,1)} %copy-done.38) | copy-start | bytes 40
  200.6 5.7 %collective-permute-start.6 = (bf16[2,12,6,576]{3,2,1,0:T(8,128)(2,1)S(1)}, bf16[2,12,6,576]{3,2,1,0:T(8,128)(2,1)S(1)}, u32[]{:S(2)}, u32[]{:S(2)}) collective-permute-start(bf16[2,12,6,576]{3,2,1,0:T(8,128)(2,1)S(1)} %get-tuple-element.34), channel_id=1, source_target_pairs={{4,0},{8,4},{12,8},{16,12},{20,16},{24,20},{28,24},{0,28},{5,1},{9... | collective-permute-start | bytes 497672 | tf_op jit(solution)/shard_map/ppermute | solution.py:32
  206.4 5.6 %collective-permute-start.7 = (bf16[2,3,12,576]{3,2,1,0:T(8,128)(2,1)S(1)}, bf16[2,3,12,576]{3,2,1,0:T(8,128)(2,1)S(1)}, u32[]{:S(2)}, u32[]{:S(2)}) collective-permute-start(bf16[2,3,12,576]{3,2,1,0:T(8,128)(2,1)S(1)} %pad_maximum_fusion.7), channel_id=1, source_target_pairs={{1,0},{2,1},{3,2},{5,4},{6,5},{7,6},{9,8},{10,9},{11,10},{13,12},{... | collective-permute-start | bytes 248840 | tf_op jit(solution)/shard_map/ppermute | solution.py:26
  (28 other events, 44.4 us)
where the time goes:
time: 282 us; the launch traced here: 278 us
  local copies, waits for them, and re-layouts  125 us (44%)
  blocking collectives  61.7 us (22%)
  other arithmetic  32.3 us (11%)
  matrix products  20.3 us (7%)
  starting transfers between devices  17.4 us (6%)
  waiting for transfers between devices  14.8 us (5%)
  between operations  6.7 us (2%)
    psum x1, blocking collectives, per_device(): lax.psum((qkv_total, proj_total, up_total, down_total), ('lon', 'lat'))  61.7 us
    gather x1, local copies, waits for them, and re-layouts, window_terms(): gathered = table_rows[:, :, :, bias_index].astype(jnp.float32)  51.2 us
    convert_element_type x1, local copies, waits for them, and re-layouts, window_terms(): gathered = table_rows[:, :, :, bias_index].astype(jnp.float32)  31.1 us
    ppermute x4, starting transfers between devices, from_behind(): return lax.ppermute(x, axis, pairs)  11.6 us
    convert_element_type x1, other arithmetic, window_terms(): gathered = table_rows[:, :, :, bias_index].astype(jnp.float32)  11.4 us
    ppermute x4, waiting for transfers between devices, from_behind(): return lax.ppermute(x, axis, pairs)  8.96 us
    unnamed x91, local copies, waits for them, and re-layouts  8.48 us
    dot_general x9, matrix products, product(): return jnp.dot(left, right, preferred_element_type=jnp.float32)  8.22 us
  transfers between devices with their start and end apart: 8, of which 5 were waited for; matrix products, arithmetic and copies ran while one was open for 41% of the time, Pallas kernels for 0%

commit v1 on v0

v1 whole, which is shorter than its diff:
```python
import functools
import math

import jax
import jax.numpy as jnp
from jax import lax
from jax.experimental import pallas as pl
from jax.experimental.pallas import tpu as pltpu
from jax.sharding import PartitionSpec as P

C = 192
HEADS = 6
FF = 768
HEAD_DIM = 32
WLAT = 6
WLON = 12
LAT_PAD = 11
WTOK = 144
HALF = 72
LANES = 128
EPSILON = 1e-05
MASKED = -1000000000.0
F32 = jnp.float32
BF16 = jnp.bfloat16


def shifted(block, axis, by, wrap):
    count = lax.axis_size(axis)
    route = [(i, (i + by) % count) for i in range(count) if wrap or 0 <= i + by < count]
    return lax.ppermute(block, axis, route)


def pull_rim(source):
    lat_part = shifted(source[:, -(WLAT // 2) :], "lat", 1, False)
    upper = jnp.concatenate([lat_part, source[:, : -(WLAT // 2)]], axis=1)
    lon_part = shifted(upper[:, :, -(WLON // 2) :], "lon", 1, True)
    return jnp.concatenate([lon_part, upper[:, :, : -(WLON // 2)]], axis=2)


def push_rim(frame):
    lon_part = shifted(frame[:, :, : WLON // 2], "lon", -1, True)
    upper = jnp.concatenate([frame[:, :, WLON // 2 :], lon_part], axis=2)
    lat_part = shifted(upper[:, : WLAT // 2], "lat", -1, False)
    return jnp.concatenate([upper[:, WLAT // 2 :], lat_part], axis=1)


def nn(left, right):
    return lax.dot_general(left, right, (((1,), (0,)), ((), ())), preferred_element_type=F32)


def nt(left, right):
    return lax.dot_general(left, right, (((1,), (1,)), ((), ())), preferred_element_type=F32)


def tn(left, right):
    return lax.dot_general(left, right, (((0,), (0,)), ((), ())), preferred_element_type=F32)


def gather_kernel(pieces, index_ref, table_ref, out_ref):
    index = index_ref[...]
    low = jnp.bitwise_and(index, LANES - 1)
    high = jnp.right_shift(index, 7)

    def one_row(r, carry):
        total = jnp.zeros(index.shape, F32)
        for piece in range(pieces):
            source = jnp.broadcast_to(table_ref[r, pl.ds(piece, 1), :], index.shape)
            found = jnp.take_along_axis(source, low, axis=1, mode="promise_in_bounds")
            total = jnp.where(high == piece, found, total)
        out_ref[r] = total
        return carry

    lax.fori_loop(0, table_ref.shape[0], one_row, 0)


def center_of(values):
    center = values - jnp.mean(values, axis=-1, keepdims=True)
    spread = jnp.mean(center * center, axis=-1, keepdims=True)
    return center, lax.rsqrt(spread + EPSILON)


def norm_back(center, scale, upstream):
    inner = jnp.mean(upstream * center, axis=-1, keepdims=True)
    outer = jnp.mean(upstream, axis=-1, keepdims=True)
    return scale * (upstream - outer - center * (scale * scale * inner))


def block_kernel(
    window_rows,
    edges_ref,
    bits_ref,
    scales_ref,
    start_ref,
    d_out_ref,
    qkv_ref,
    proj_ref,
    up_ref,
    down_ref,
    bias_ref,
    final_ref,
    grad_ref,
    qkv_total_ref,
    proj_total_ref,
    up_total_ref,
    down_total_ref,
    heads_s,
    dq_s,
    dk_s,
    dv_s,
):
    def dequant(codes, layer, fan_in):
        largest = jnp.left_shift(jnp.int32(1), bits_ref[layer] - 1) - 1
        scale = jnp.full((1, codes.shape[1]), scales_ref[layer].astype(F32), F32)
        factor = math.sqrt(C / fan_in) / scale
        return (jnp.clip(codes, -largest, largest).astype(F32) * factor).astype(BF16)

    w_q = dequant(qkv_ref[:, :C], 0, C)
    w_k = dequant(qkv_ref[:, C : 2 * C], 0, C)
    w_v = dequant(qkv_ref[:, 2 * C :], 0, C)
    w_proj = dequant(proj_ref[...], 1, C)
    start = start_ref[...].astype(F32)
    center, inverse = center_of(start)
    normed = (center * inverse).astype(BF16)
    q = nn(normed, w_q).astype(BF16)
    k = nn(normed, w_k).astype(BF16)
    v = nn(normed, w_v).astype(BF16)

    lane = lax.broadcasted_iota(jnp.int32, (HALF, C), 1)
    head_masks = [(lane >= h * HEAD_DIM) & (lane < (h + 1) * HEAD_DIM) for h in range(HEADS)]

    def stack(values):
        wide = values.astype(F32)
        return jnp.concatenate([jnp.where(m, wide, 0.0) for m in head_masks], axis=0).astype(BF16)

    def unstack(values):
        total = jnp.zeros((HALF, C), F32)
        for h, m in enumerate(head_masks):
            total = jnp.where(m, values[h * HALF : (h + 1) * HALF], total)
        return total

    keys = lax.broadcasted_iota(jnp.int32, (HEADS * HALF, HALF), 1)
    blocks = start.shape[0] // HALF
    saved = []
    for b in range(blocks):
        level, a = b // window_rows, b % window_rows
        part = slice(b * HALF, (b + 1) * HALF)
        stacked_q = stack(q[part])
        bias = bias_ref[a * HEADS : (a + 1) * HEADS, (1 - level) * HALF : (2 - level) * HALF, :]
        bias = bias.reshape(HEADS * HALF, LANES)[:, :HALF]
        scores = nt(stacked_q, k[part]) * HEAD_DIM ** (-0.5) + bias
        allowed = (keys >= edges_ref[2 * a]) & (keys < edges_ref[2 * a + 1])
        scores = jnp.where(allowed, scores, MASKED)
        weights = jnp.exp(scores - jnp.max(scores, axis=-1, keepdims=True))
        weights = weights / jnp.sum(weights, axis=-1, keepdims=True)
        saved.append((stacked_q, weights, allowed))
        heads_s[part, :] = unstack(nn(weights.astype(BF16), v[part]))

    heads = heads_s[...].astype(BF16)
    resid = (start + nn(heads, w_proj)).astype(BF16)
    center_two, inverse_two = center_of(resid.astype(F32))
    normed_two = (center_two * inverse_two).astype(BF16)
    w_up = dequant(up_ref[...], 2, C)
    w_down = dequant(down_ref[...], 3, FF)
    pre = nn(normed_two, w_up)
    cubic = math.sqrt(2 / math.pi)
    square = pre * pre
    bent = jnp.tanh(cubic * (pre + 0.044715 * square * pre))
    hidden = (0.5 * pre * (1.0 + bent)).astype(BF16)
    final_ref[...] = (resid.astype(F32) + nn(hidden, w_down)).astype(BF16)
    d_out = d_out_ref[...]
    down_total_ref[...] = tn(hidden, d_out).astype(BF16)
    d_hidden = nt(d_out, w_down).astype(BF16).astype(F32)
    slope = 0.5 * (1.0 + bent) + 0.5 * pre * (1.0 - bent * bent) * cubic * (
        1.0 + 3 * 0.044715 * square
    )
    d_pre = (slope * d_hidden).astype(BF16)
    up_total_ref[...] = tn(normed_two, d_pre).astype(BF16)
    d_normed_two = nt(d_pre, w_up).astype(BF16).astype(F32)
    d_resid = (d_out.astype(F32) + norm_back(center_two, inverse_two, d_normed_two)).astype(BF16)
    proj_total_ref[...] = tn(heads, d_resid).astype(BF16)
    d_heads = nt(d_resid, w_proj).astype(BF16)

    for b in range(blocks):
        part = slice(b * HALF, (b + 1) * HALF)
        stacked_q, weights, allowed = saved[b]
        d_stacked = stack(d_heads[part])
        d_weights = nt(d_stacked, v[part]).astype(BF16).astype(F32)
        dv_s[part, :] = tn(weights.astype(BF16), d_stacked)
        inner = jnp.sum(weights * d_weights, axis=-1, keepdims=True)
        d_scores = jnp.where(allowed, weights * (d_weights - inner), 0.0)
        d_scores = (d_scores * HEAD_DIM ** (-0.5)).astype(BF16)
        dq_s[part, :] = unstack(nn(d_scores, k[part]))
        dk_s[part, :] = tn(d_scores, stacked_q)

    dq = dq_s[...].astype(BF16)
    dk = dk_s[...].astype(BF16)
    dv = dv_s[...].astype(BF16)
    qkv_total_ref[:, :C] = tn(normed, dq).astype(BF16)
    qkv_total_ref[:, C : 2 * C] = tn(normed, dk).astype(BF16)
    qkv_total_ref[:, 2 * C :] = tn(normed, dv).astype(BF16)
    d_normed = (nt(dq, w_q) + nt(dk, w_k) + nt(dv, w_v)).astype(BF16).astype(F32)
    grad_ref[...] = (d_resid.astype(F32) + norm_back(center, inverse, d_normed)).astype(BF16)


def merge_patches(final, merge_weight):
    level_count, row_count, col_count, feat_count = final.shape
    grouped = final.reshape(level_count, row_count // 2, 2, col_count // 2, 2, feat_count)
    grouped = grouped.transpose(0, 1, 3, 2, 4, 5).reshape(-1, 4 * feat_count)
    center, inverse = center_of(grouped.astype(F32))
    merged = nn((center * inverse).astype(BF16), merge_weight).astype(BF16)
    return merged.reshape(level_count, row_count // 2, col_count // 2, 2 * feat_count)


def per_device(
    tokens,
    cotangent,
    qkv_codes,
    proj_codes,
    up_codes,
    down_codes,
    bit_widths,
    quant_scales,
    bias_table,
    bias_index,
    merge_weight,
):
    level_count, row_count, col_count, feat_count = tokens.shape
    token_count = level_count * row_count * col_count
    window_rows = row_count // WLAT
    grid_shape = (level_count, row_count, col_count)
    lat_limit = lax.axis_size("lat") * row_count - LAT_PAD
    lat_index = lax.axis_index("lat")
    lat_start = lat_index * row_count - WLAT // 2
    row_ids = lat_index * row_count + jnp.arange(row_count, dtype=jnp.int32)
    row_mask = (row_ids < lat_limit)[None, :, None, None]

    both = jnp.concatenate([tokens, cotangent], axis=-1)
    both = jnp.where(row_mask, both, jnp.zeros_like(both))
    frame = pull_rim(both).reshape(token_count, 2 * feat_count)

    pair = bias_index.reshape(2, HALF, 2, HALF)
    index = jnp.concatenate([pair[0, :, 0], pair[1, :, 1]], axis=0)
    index = jnp.pad(index, ((0, 0), (0, LANES - HALF)))
    positions = bias_table.shape[-1]
    pieces = -(-positions // LANES)
    table = bias_table.reshape(window_rows * HEADS, positions).astype(F32)
    table = jnp.pad(table, ((0, 0), (0, pieces * LANES - positions)))
    table = table.reshape(window_rows * HEADS, pieces, LANES)
    vmem = pl.BlockSpec(memory_space=pltpu.VMEM)
    smem = pl.BlockSpec(memory_space=pltpu.SMEM)
    bias = pl.pallas_call(
        functools.partial(gather_kernel, pieces),
        out_shape=jax.ShapeDtypeStruct((window_rows * HEADS, WTOK, LANES), F32),
        in_specs=[vmem, vmem],
        out_specs=vmem,
        compiler_params=pltpu.CompilerParams(vmem_limit_bytes=32 * 2**20),
        cost_estimate=pl.CostEstimate(flops=10**9, bytes_accessed=4 * 10**6, transcendentals=0),
        name="bias_gather",
    )(index, table)

    first_row = lat_start + WLAT * jnp.arange(window_rows, dtype=jnp.int32)
    edges = jnp.stack([-first_row * WLON, (lat_limit - first_row) * WLON], axis=1).reshape(-1)
    wide = jax.ShapeDtypeStruct((token_count, feat_count), BF16)
    final, grad, qkv_total, proj_total, up_total, down_total = pl.pallas_call(
        functools.partial(block_kernel, window_rows),
        out_shape=[
            wide,
            wide,
            jax.ShapeDtypeStruct((C, 3 * C), BF16),
            jax.ShapeDtypeStruct((C, C), BF16),
            jax.ShapeDtypeStruct((C, FF), BF16),
            jax.ShapeDtypeStruct((FF, C), BF16),
        ],
        in_specs=[smem] * 3 + [vmem] * 7,
        out_specs=[vmem] * 6,
        scratch_shapes=[pltpu.VMEM((token_count, feat_count), F32)] * 4,
        compiler_params=pltpu.CompilerParams(vmem_limit_bytes=48 * 2**20),
        name="block",
    )(
        edges,
        bit_widths,
        quant_scales,
        frame[:, :feat_count],
        frame[:, feat_count:],
        qkv_codes,
        proj_codes,
        up_codes,
        down_codes,
        bias,
    )
    summed = lax.psum((qkv_total, proj_total, up_total, down_total), ("lon", "lat"))
    owned = push_rim(jnp.concatenate([final, grad], axis=-1).reshape(grid_shape + (-1,)))
    owned = jnp.where(row_mask, owned, jnp.zeros_like(owned))
    merged = merge_patches(owned[..., :feat_count], merge_weight)
    return (merged, owned[..., feat_count:]) + tuple(summed)


def solution(mesh):
    split = P(None, "lat", "lon", None)
    placed = (split, split, P(), P(), P(), P(), P(), P(), P("lat", None, None, None), P(), P())
    return jax.shard_map(
        per_device,
        mesh=mesh,
        in_specs=placed,
        out_specs=(split, split, P(), P(), P(), P()),
        check_vma=False,
    )
```

time: 282 us -> 193 us (0.68)
  waiting for transfers between devices: 14.8 us -> 128 us
  local copies, waits for them, and re-layouts: 125 us -> 13.3 us
  blocking collectives: 61.7 us -> 0 us
  other arithmetic: 32.3 us -> 3.73 us
  Pallas kernels: 0 us -> 23.8 us
  matrix products: 20.3 us -> 0.28 us
  starting transfers between devices: 17.4 us -> 7.95 us
  between operations: 6.7 us -> 14.4 us
    psum x0 -> x1, waiting for transfers between devices: none -> 117 us  [per_device(): lax.psum((qkv_total, proj_total, up_total, down_total), ('lon', 'lat'))]
    psum x1 -> x0, blocking collectives: 61.7 us -> none  [per_device(): lax.psum((qkv_total, proj_total, up_total, down_total), ('lon', 'lat'))]
    gather x1 -> x0, local copies, waits for them, and re-layouts: 51.2 us -> none  [window_terms(): gathered = table_rows[:, :, :, bias_index].astype(jnp.float32)]
    convert_element_type x5 -> x4, local copies, waits for them, and re-layouts: 37.4 us -> 0.72 us  [the longest x3 0.66 us: merge_patches(): center, inverse = center_of(grouped.astype(F32))]
    pallas_call x0 -> x2, Pallas kernels: none -> 23.8 us  [the longest x1 16.6 us: per_device(): pl.pallas_call(functools.partial(gather_kernel, pieces), out_shape=jax.Sh...]
    dot_general x19 -> x1, matrix products: 20.3 us -> 0.28 us  [nn(): lax.dot_general(left, right, (((1,), (0,)), ((), ())), preferred_element_...]
    convert_element_type x5 -> x0, other arithmetic: 13.5 us -> none  [the longest x1 11.4 us: window_terms(): gathered = table_rows[:, :, :, bias_index].astype(jnp.float32)]
    ppermute x8 -> x4, starting transfers between devices: 17.4 us -> 7.92 us  [shifted(): return lax.ppermute(block, axis, route)]
  transfers between devices with their start and end apart: 8 -> 5, of which waited for: 5 -> 3; matrix products, arithmetic and copies ran while one was open for 41% -> 2% of each run, Pallas kernels for 0% -> 9%
where the time goes in v1:
time: 193 us; the launch traced here: 191 us
  waiting for transfers between devices  128 us (66%)
  Pallas kernels  23.8 us (12%)
  between operations  14.4 us (7%)
  local copies, waits for them, and re-layouts  13.3 us (7%)
  starting transfers between devices  7.95 us (4%)
  other arithmetic  3.73 us (2%)
    psum x1, waiting for transfers between devices, per_device(): lax.psum((qkv_total, proj_total, up_total, down_total), ('lon', 'lat'))  117 us
    pallas_call x1, Pallas kernels, per_device(): pl.pallas_call(functools.partial(gather_kernel, pieces), out_shape=jax.Sh...  16.6 us
    ppermute x4, waiting for transfers between devices, shifted(): return lax.ppermute(block, axis, route)  10.6 us
    unnamed x40, local copies, waits for them, and re-layouts  8.57 us
    ppermute x4, starting transfers between devices, shifted(): return lax.ppermute(block, axis, route)  7.92 us
    pallas_call x1, Pallas kernels, per_device(): pl.pallas_call(functools.partial(block_kernel, window_rows), out_shape=[w...  7.28 us
  transfers between devices with their start and end apart: 5, of which 3 were waited for; matrix products, arithmetic and copies ran while one was open for 2% of the time, Pallas kernels for 9%

profile of v1, /device:TPU:1, one launch (start us, length us, event | category | flops | bytes accessed | tf_op | source)
XLA Modules:
  0.0 191.0 jit_solution(1433106094419693122)
XLA Ops:
  7.3 1.0 copy.46
  8.5 3.9 %collective-permute-start = (bf16[2,3,12,384]{3,2,1,0:T(8,128)(2,1)S(1)}, bf16[2,3,12,384]{3,2,1,0:T(8,128)(2,1)S(1)}, u32[]{:S(2)}, u32[]{:S(2)}) collective-permute-start(bf16[2,3,12,384]{3,2,1,0:T(8,128)(2,1)S(1)} %slice.56), channel_id=1, source_target_pairs={{0,1},{1,2},{2,3},{4,5},{5,6},{6,7},{8,9},{9,10},{10,11},{12,13},{... | collective-permute-start | bytes 165896 | tf_op jit(solution)/shard_map/ppermute | solution.py:30
  12.6 0.9 copy-done.13
  13.4 0.3 reshape.105
  13.9 0.7 fusion.2
  14.7 2.6 %collective-permute-start.1 = (bf16[2,12,6,384]{3,2,1,0:T(8,128)(2,1)}, bf16[2,12,6,384]{3,2,1,0:T(8,128)(2,1)}, u32[]{:S(2)}, u32[]{:S(2)}) collective-permute-start(bf16[2,12,6,384]{3,2,1,0:T(8,128)(2,1)} %fusion.2), channel_id=1, source_target_pairs={{0,4},{4,8},{8,12},{12,16},{16,20},{20,24},{24,28},{28,0},{1,5},{5... | collective-permute-start | bytes 331784 | tf_op jit(solution)/shard_map/ppermute | solution.py:30
  17.8 16.6 %bias_gather.1.bias_ref = f32[12,144,128]{2,1,0:T(8,128)S(1)} custom-call(s32[144,128]{1,0:T(8,128)S(1)} %pad.9.index_ref, f32[12,26,128]{2,1,0:T(8,128)S(1)} %reshape.111.table_ref), custom_call_target="tpu_custom_call" | custom-call | flops 1000000000 | bytes 4000000 | tf_op jit(solution)/shard_map/bias_gather/pallas_call | solution.py:251
  34.4 1.8 fusion
  36.2 1.8 reshape.104
  38.0 1.1 fusion.7
  39.1 0.6 copy-done.4
  39.7 7.3 %block.1 = (bf16[288,192]{1,0:T(8,128)(2,1)S(1)}, bf16[288,192]{1,0:T(8,128)(2,1)S(1)}, bf16[192,576]{1,0:T(8,128)(2,1)}, bf16[192,192]{1,0:T(8,128)(2,1)}, bf16...) custom-call(s32[4]{0:T(128)S(1)} %reshape.103.edges_ref, s32[4]{0:T(128)S(1)} %copy-done.4, s32[4]{0:T(128)S(1)} %copy-done.5, ...), custom_call_target="tpu_custom_call" | custom-call | tf_op jit(solution)/shard_map/block/pallas_call | solution.py:264
  47.3 4.5 %collective-permute-done.2 = bf16[2,12,6,384]{3,2,1,0:T(8,128)(2,1)S(1)} collective-permute-done((bf16[2,12,6,384]{3,2,1,0:T(8,128)(2,1)S(1)}, bf16[2,12,6,384]{3,2,1,0:T(8,128)(2,1)S(1)}, u32[]{:S(2)}, u32[]{:S(2)}) %collective-permute-start.2) | collective-permute-done | bytes 110624 | tf_op jit(solution)/shard_map/ppermute | solution.py:30
  51.9 1.3 collective-permute-start.3
  53.3 6.1 %collective-permute-done.3 = bf16[2,3,12,384]{3,2,1,0:T(8,128)(2,1)S(1)} collective-permute-done((bf16[2,3,12,384]{3,2,1,0:T(8,128)(2,1)S(1)}, bf16[2,3,12,384]{3,2,1,0:T(8,128)(2,1)S(1)}, u32[]{:S(2)}, u32[]{:S(2)}) %collective-permute-start.3) | collective-permute-done | bytes 55328 | tf_op jit(solution)/shard_map/ppermute | solution.py:30
  60.2 0.3 multiply_reduce_fusion
  60.6 0.8 copy.57
  62.1 0.3 convolution_convert_fusion
  62.4 0.7 copy.56
  63.0 116.9 %all-reduce.5.cloned.1.call-done = (bf16[192,576]{1,0:T(8,128)(2,1)}, bf16[192,192]{1,0:T(8,128)(2,1)}, bf16[192,768]{1,0:T(8,128)(2,1)}, bf16[768,192]{1,0:T(8,128)(2,1)}) async-done(((bf16[192,576]{1,0:T(8,128)(2,1)}, bf16[192,192]{1,0:T(8,128)(2,1)}, bf16[192,768]{1,0:T(8,128)(2,1)}, bf16[768,192]{1,0:T(8,128)(2,1)}), (bf16[192,576]{1,0:T(8,128)(2,1)}, bf16[192,192]{1,0:T(8,128)(2,1)}, ...) | async-done | bytes 884752 | tf_op jit(solution)/shard_map/psum | solution.py:291
  179.9 1.9 copy.58
  181.9 0.7 copy.65
  182.8 0.6 copy.66
  183.5 0.7 copy.67
  (67 shorter events, 3.2 us)
Async XLA Ops:
  7.2 54.9 %copy-start = (bf16[768,384]{1,0:T(8,128)(2,1)S(1)}, bf16[768,384]{1,0:T(8,128)(2,1)}, u32[]{:S(2)}) copy-start(bf16[768,384]{1,0:T(8,128)(2,1)} %param.21) | copy-start | bytes 1769476
  7.2 172.8 %all-reduce.5.cloned.1.call-start = ((), (), s32[]{:S(2)}) async-start(), calls=%async_computation | async-start | bytes 2064384 | tf_op jit(solution)/shard_map/psum | solution.py:291
  7.2 1.0 copy-start.11
  8.5 4.0 %copy-start.14 = (bf16[2,1,6,3312]{3,0,2,1:T(2,128)(2,1)S(1)}, bf16[2,1,6,3312]{3,0,2,1:T(2,128)(2,1)}, u32[]{:S(2)}) copy-start(bf16[2,1,6,3312]{3,0,2,1:T(2,128)(2,1)} %param.19) | copy-start | bytes 238468
  8.5 5.4 %collective-permute-start = (bf16[2,3,12,384]{3,2,1,0:T(8,128)(2,1)S(1)}, bf16[2,3,12,384]{3,2,1,0:T(8,128)(2,1)S(1)}, u32[]{:S(2)}, u32[]{:S(2)}) collective-permute-start(bf16[2,3,12,384]{3,2,1,0:T(8,128)(2,1)S(1)} %slice.56), channel_id=1, source_target_pairs={{0,1},{1,2},{2,3},{4,5},{5,6},{6,7},{8,9},{9,10},{10,11},{12,13},{... | collective-permute-start | bytes 165896 | tf_op jit(solution)/shard_map/ppermute | solution.py:30
  12.5 0.9 copy-start.13
  13.9 3.6 %copy-start.6 = (s32[768,192]{0,1:T(8,128)S(1)}, s32[768,192]{0,1:T(8,128)}, u32[]{:S(2)}) copy-start(s32[768,192]{0,1:T(8,128)} %param.16) | copy-start | bytes 1769476
  13.9 0.7 copy-start.7
  14.7 19.7 %collective-permute-start.1 = (bf16[2,12,6,384]{3,2,1,0:T(8,128)(2,1)}, bf16[2,12,6,384]{3,2,1,0:T(8,128)(2,1)}, u32[]{:S(2)}, u32[]{:S(2)}) collective-permute-start(bf16[2,12,6,384]{3,2,1,0:T(8,128)(2,1)} %fusion.2), channel_id=1, source_target_pairs={{0,4},{4,8},{8,12},{12,16},{16,20},{20,24},{24,28},{28,0},{1,5},{5... | collective-permute-start | bytes 331784 | tf_op jit(solution)/shard_map/ppermute | solution.py:30
  17.8 16.6 %copy-start.8 = (bf16[2,3,12,384]{3,2,1,0:T(8,128)(2,1)S(1)}, bf16[2,3,12,384]{3,2,1,0:T(8,128)(2,1)}, u32[]{:S(2)}) copy-start(bf16[2,3,12,384]{3,2,1,0:T(8,128)(2,1)} %copy-done.7) | copy-start | bytes 165892
  34.4 4.7 %copy-start.3 = (s32[192,192]{1,0:T(8,128)S(1)}, s32[192,192]{1,0:T(8,128)}, u32[]{:S(2)}) copy-start(s32[192,192]{1,0:T(8,128)} %proj_ref.1) | copy-start | bytes 442372
  36.2 2.9 %copy-start.1 = (s32[192,768]{1,0:T(8,128)S(1)}, s32[192,768]{1,0:T(8,128)}, u32[]{:S(2)}) copy-start(s32[192,768]{1,0:T(8,128)} %up_ref.1) | copy-start | bytes 1769476
  36.2 2.9 %copy-start.2 = (s32[192,576]{1,0:T(8,128)S(1)}, s32[192,576]{1,0:T(8,128)}, u32[]{:S(2)}) copy-start(s32[192,576]{1,0:T(8,128)} %qkv_ref.1) | copy-start | bytes 1327108
  39.1 0.7 copy-start.4
  39.1 0.7 copy-start.5
  47.3 4.6 %collective-permute-start.2 = (bf16[2,12,6,384]{3,2,1,0:T(8,128)(2,1)S(1)}, bf16[2,12,6,384]{3,2,1,0:T(8,128)(2,1)S(1)}, u32[]{:S(2)}, u32[]{:S(2)}) collective-permute-start(bf16[2,12,6,384]{3,2,1,0:T(8,128)(2,1)S(1)} %get-tuple-element.49), channel_id=1, source_target_pairs={{0,28},{4,0},{8,4},{12,8},{16,12},{20,16},{24,20},{28,24},{1,29},{... | collective-permute-start | bytes 331784 | tf_op jit(solution)/shard_map/ppermute | solution.py:30
  51.9 7.4 %collective-permute-start.3 = (bf16[2,3,12,384]{3,2,1,0:T(8,128)(2,1)S(1)}, bf16[2,3,12,384]{3,2,1,0:T(8,128)(2,1)S(1)}, u32[]{:S(2)}, u32[]{:S(2)}) collective-permute-start(bf16[2,3,12,384]{3,2,1,0:T(8,128)(2,1)S(1)} %pad_maximum_fusion.2), channel_id=1, source_target_pairs={{1,0},{2,1},{3,2},{5,4},{6,5},{7,6},{9,8},{10,9},{11,10},{13,12},{... | collective-permute-start | bytes 165896 | tf_op jit(solution)/shard_map/ppermute | solution.py:30
  179.9 1.9 %copy-start.10 = (bf16[192,576]{1,0:T(8,128)(2,1)S(1)}, bf16[192,576]{1,0:T(8,128)(2,1)}, u32[]{:S(2)}) copy-start(bf16[192,576]{1,0:T(8,128)(2,1)} %get-tuple-element.58) | copy-start | bytes 663556
  181.9 1.0 copy-start.12
  181.9 1.6 copy-start.9
Sparse Core Ops, SparseCore 0:
  47.5 132.4 all-reduce.4

commit v2 on v1

--- a/solution.py
+++ b/solution.py
@@ -20,6 +20,10 @@
 LANES = 128
 EPSILON = 1e-05
 MASKED = -1000000000.0
+UP_AT = 6 * C
+DOWN_AT = 12 * C
+PAIR_AT = 16 * C
+TOTAL_ROWS = 18 * C
 F32 = jnp.float32
 BF16 = jnp.bfloat16
 
@@ -35,13 +39,6 @@
     upper = jnp.concatenate([lat_part, source[:, : -(WLAT // 2)]], axis=1)
     lon_part = shifted(upper[:, :, -(WLON // 2) :], "lon", 1, True)
     return jnp.concatenate([lon_part, upper[:, :, : -(WLON // 2)]], axis=2)
-
-
-def push_rim(frame):
-    lon_part = shifted(frame[:, :, : WLON // 2], "lon", -1, True)
-    upper = jnp.concatenate([frame[:, :, WLON // 2 :], lon_part], axis=2)
-    lat_part = shifted(upper[:, : WLAT // 2], "lat", -1, False)
-    return jnp.concatenate([upper[:, WLAT // 2 :], lat_part], axis=1)
 
 
 def nn(left, right):
@@ -99,14 +96,13 @@
     bias_ref,
     final_ref,
     grad_ref,
-    qkv_total_ref,
-    proj_total_ref,
-    up_total_ref,
-    down_total_ref,
+    totals_ref,
     heads_s,
     dq_s,
     dk_s,
     dv_s,
+    narrow_s,
+    pair_s,
 ):
     def dequant(codes, layer, fan_in):
         largest = jnp.left_shift(jnp.int32(1), bits_ref[layer] - 1) - 1
@@ -168,16 +164,22 @@
     hidden = (0.5 * pre * (1.0 + bent)).astype(BF16)
     final_ref[...] = (resid.astype(F32) + nn(hidden, w_down)).astype(BF16)
     d_out = d_out_ref[...]
-    down_total_ref[...] = tn(hidden, d_out).astype(BF16)
+    down_total = tn(hidden, d_out)
+    totals_ref[DOWN_AT : DOWN_AT + FF, :] = down_total[:, :LANES].astype(BF16)
+    pair_s[:, : C - LANES] = down_total[: FF // 2, LANES:]
+    pair_s[:, C - LANES :] = down_total[FF // 2 :, LANES:]
+    totals_ref[PAIR_AT : PAIR_AT + FF // 2, :] = pair_s[...].astype(BF16)
     d_hidden = nt(d_out, w_down).astype(BF16).astype(F32)
     slope = 0.5 * (1.0 + bent) + 0.5 * pre * (1.0 - bent * bent) * cubic * (
         1.0 + 3 * 0.044715 * square
     )
     d_pre = (slope * d_hidden).astype(BF16)
-    up_total_ref[...] = tn(normed_two, d_pre).astype(BF16)
+    up_total = tn(normed_two, d_pre).astype(BF16)
+    for t in range(FF // LANES):
+        totals_ref[UP_AT + t * C : UP_AT + (t + 1) * C, :] = up_total[:, t * LANES : (t + 1) * LANES]
     d_normed_two = nt(d_pre, w_up).astype(BF16).astype(F32)
     d_resid = (d_out.astype(F32) + norm_back(center_two, inverse_two, d_normed_two)).astype(BF16)
-    proj_total_ref[...] = tn(heads, d_resid).astype(BF16)
+    narrow_s[:, 3 * C :] = tn(heads, d_resid)
     d_heads = nt(d_resid, w_proj).astype(BF16)
 
     for b in range(blocks):
@@ -195,11 +197,150 @@
     dq = dq_s[...].astype(BF16)
     dk = dk_s[...].astype(BF16)
     dv = dv_s[...].astype(BF16)
-    qkv_total_ref[:, :C] = tn(normed, dq).astype(BF16)
-    qkv_total_ref[:, C : 2 * C] = tn(normed, dk).astype(BF16)
-    qkv_total_ref[:, 2 * C :] = tn(normed, dv).astype(BF16)
+    narrow_s[:, :C] = tn(normed, dq)
+    narrow_s[:, C : 2 * C] = tn(normed, dk)
+    narrow_s[:, 2 * C : 3 * C] = tn(normed, dv)
+    for t in range(4 * C // LANES):
+        tile = narrow_s[:, t * LANES : (t + 1) * LANES]
+        totals_ref[t * C : (t + 1) * C, :] = tile.astype(BF16)
+    spare = totals_ref.shape[0] - TOTAL_ROWS
+    if spare:
+        totals_ref[TOTAL_ROWS:, :] = jnp.zeros((spare, LANES), BF16)
     d_normed = (nt(dq, w_q) + nt(dk, w_k) + nt(dv, w_v)).astype(BF16).astype(F32)
     grad_ref[...] = (d_resid.astype(F32) + norm_back(center, inverse, d_normed)).astype(BF16)
+
+
+def reduce_kernel(
+    lon_count,
+    lat_count,
+    rim_parts,
+    totals_ref,
+    rim_ref,
+    grad_qkv_ref,
+    grad_proj_ref,
+    grad_up_ref,
+    grad_down_ref,
+    rim_out_ref,
+    core_in,
+    lat_in,
+    far_in,
+    half_s,
+    part_s,
+    result,
+    rim_in,
+    narrow_s,
+    sends,
+    receives,
+):
+    lon, lat = lax.axis_index("lon"), lax.axis_index("lat")
+    core, far, far_count = lax.rem(lon, 2), lon // 2, lon_count // 2
+    half = result.shape[0] // 2
+    part = half // lat_count
+    chunk = part // far_count
+
+    def across(distance):
+        return {"lon": lon, "lat": lax.rem(lat + distance + lat_count, lat_count)}
+
+    def along(distance):
+        other = lax.rem(far + distance + far_count, far_count)
+        return {"lon": other * 2 + core, "lat": lat}
+
+    twin = {"lon": far * 2 + 1 - core, "lat": lat}
+    west, east = lax.rem(lon + lon_count - 1, lon_count), lax.rem(lon + 1, lon_count)
+    north, south = lax.rem(lat + lat_count - 1, lat_count), lax.rem(lat + 1, lat_count)
+    rim_to = [
+        {"lon": west, "lat": lat},
+        {"lon": lon, "lat": north},
+        {"lon": west, "lat": north},
+    ]
+    rim_from = [
+        {"lon": east, "lat": lat},
+        {"lon": lon, "lat": south},
+        {"lon": east, "lat": south},
+    ]
+    greeted = [twin] + [across(d) for d in range(1, lat_count)]
+    greeted += [along(d) for d in range(1, far_count)] + rim_to + rim_from
+    barrier = pltpu.get_barrier_semaphore()
+    for device in greeted:
+        pl.semaphore_signal(barrier, inc=1, device_id=device, device_id_type=pl.DeviceIdType.MESH)
+    pl.semaphore_wait(barrier, len(greeted))
+
+    used = []
+
+    def send(source, target, device):
+        slot = len(used)
+        copy = pltpu.make_async_remote_copy(
+            src_ref=source,
+            dst_ref=target,
+            send_sem=sends.at[slot],
+            recv_sem=receives.at[slot],
+            device_id=device,
+            device_id_type=pl.DeviceIdType.MESH,
+        )
+        copy.start()
+        used.append(copy)
+        return copy
+
+    def rows(index, size):
+        return pl.ds(pl.multiple_of(index * size, 16), size)
+
+    first = send(totals_ref.at[rows(1 - core, half)], core_in, twin)
+    rims = []
+    at = 0
+    for length, device in zip(rim_parts, rim_to):
+        window = pl.ds(at, length)
+        rims.append(send(rim_ref.at[window], rim_in.at[window], device))
+        at += length
+    first.wait_recv()
+    half_s[...] = (totals_ref[rows(core, half), :].astype(F32) + core_in[...].astype(F32)).astype(BF16)
+
+    copies = []
+    for d in range(1, lat_count):
+        target = lax.rem(lat + d, lat_count)
+        copies.append(send(half_s.at[rows(target, part)], lat_in.at[d - 1], across(d)))
+    total = half_s[rows(lat, part), :].astype(F32)
+    for d, copy in enumerate(copies):
+        copy.wait_recv()
+        total = total + lat_in[d].astype(F32)
+    part_s[...] = total.astype(BF16)
+
+    copies = []
+    for d in range(1, far_count):
+        target = lax.rem(far + d, far_count)
+        copies.append(send(part_s.at[rows(target, chunk)], far_in.at[d - 1], along(d)))
+    total = part_s[rows(far, chunk), :].astype(F32)
+    for d, copy in enumerate(copies):
+        copy.wait_recv()
+        total = total + far_in[d].astype(F32)
+    mine = rows((core * lat_count + lat) * far_count + far, chunk)
+    result[mine, :] = total.astype(BF16)
+
+    copies = [send(result.at[mine], result.at[mine], along(d)) for d in range(1, far_count)]
+    for copy in copies:
+        copy.wait_recv()
+    mine = rows(core * lat_count + lat, part)
+    copies = [send(result.at[mine], result.at[mine], across(d)) for d in range(1, lat_count)]
+    for copy in copies:
+        copy.wait_recv()
+    mine = rows(core, half)
+    last = send(result.at[mine], result.at[mine], twin)
+    for copy in rims:
+        copy.wait_recv()
+    rim_out_ref[...] = rim_in[...]
+    last.wait_recv()
+
+    for t in range(4 * C // LANES):
+        narrow_s[:, t * LANES : (t + 1) * LANES] = result[t * C : (t + 1) * C, :].astype(F32)
+    grad_qkv_ref[...] = narrow_s[:, : 3 * C].astype(BF16)
+    grad_proj_ref[...] = narrow_s[:, 3 * C :].astype(BF16)
+    for t in range(FF // LANES):
+        grad_up_ref[:, t * LANES : (t + 1) * LANES] = result[UP_AT + t * C : UP_AT + (t + 1) * C, :]
+    grad_down_ref[:, :LANES] = result[DOWN_AT : DOWN_AT + FF, :]
+    pair = result[PAIR_AT : PAIR_AT + FF // 2, :].astype(F32)
+    grad_down_ref[: FF // 2, LANES:] = pair[:, : C - LANES].astype(BF16)
+    grad_down_ref[FF // 2 :, LANES:] = pair[:, C - LANES :].astype(BF16)
+    for copy in used:
+        copy.wait_send()
 
 
 def merge_patches(final, merge_weight):
@@ -261,19 +402,16 @@
     first_row = lat_start + WLAT * jnp.arange(window_rows, dtype=jnp.int32)
     edges = jnp.stack([-first_row * WLON, (lat_limit - first_row) * WLON], axis=1).reshape(-1)
     wide = jax.ShapeDtypeStruct((token_count, feat_count), BF16)
-    final, grad, qkv_total, proj_total, up_total, down_total = pl.pallas_call(
+    lon_count, lat_count = lax.axis_size("lon"), lax.axis_size("lat")
+    chunk = -(-TOTAL_ROWS // (lon_count * lat_count * 16)) * 16
+    total_rows = chunk * lon_count * lat_count
+    final, grad, totals = pl.pallas_call(
         functools.partial(block_kernel, window_rows),
-        out_shape=[
-            wide,
-            wide,
-            jax.ShapeDtypeStruct((C, 3 * C), BF16),
-            jax.ShapeDtypeStruct((C, C), BF16),
-            jax.ShapeDtypeStruct((C, FF), BF16),
-            jax.ShapeDtypeStruct((FF, C), BF16),
-        ],
+        out_shape=[wide, wide, jax.ShapeDtypeStruct((total_rows, LANES), BF16)],
         in_specs=[smem] * 3 + [vmem] * 7,
-        out_specs=[vmem] * 6,
-        scratch_shapes=[pltpu.VMEM((token_count, feat_count), F32)] * 4,
+        out_specs=[vmem] * 3,
+        scratch_shapes=[pltpu.VMEM((token_count, feat_count), F32)] * 4
+        + [pltpu.VMEM((C, 4 * C), F32), pltpu.VMEM((FF // 2, LANES), F32)],
         compiler_params=pltpu.CompilerParams(vmem_limit_bytes=48 * 2**20),
         name="block",
     )(
@@ -288,11 +426,60 @@
         down_codes,
         bias,
     )
-    summed = lax.psum((qkv_total, proj_total, up_total, down_total), ("lon", "lat"))
-    owned = push_rim(jnp.concatenate([final, grad], axis=-1).reshape(grid_shape + (-1,)))
+    frame = jnp.concatenate([final, grad], axis=-1).reshape(grid_shape + (-1,))
+    rim_rows, rim_cols = WLAT // 2, WLON // 2
+    cuts = [
+        frame[:, rim_rows:, :rim_cols],
+        frame[:, :rim_rows, rim_cols:],
+        frame[:, :rim_rows, :rim_cols],
+    ]
+    flat = [cut.reshape(-1, 2 * feat_count) for cut in cuts]
+    lengths = [-(-cut.shape[0] // 16) * 16 for cut in flat]
+    rim = jnp.concatenate(
+        [jnp.pad(cut, ((0, n - cut.shape[0]), (0, 0))) for cut, n in zip(flat, lengths)], axis=0
+    )
+    copies = 2 * (1 + lat_count - 1 + lon_count // 2 - 1) + len(cuts)
+    half = total_rows // 2
+    part = half // lat_count
+    *grads, rim = pl.pallas_call(
+        functools.partial(reduce_kernel, lon_count, lat_count, lengths),
+        out_shape=[
+            jax.ShapeDtypeStruct((C, 3 * C), BF16),
+            jax.ShapeDtypeStruct((C, C), BF16),
+            jax.ShapeDtypeStruct((C, FF), BF16),
+            jax.ShapeDtypeStruct((FF, C), BF16),
+            jax.ShapeDtypeStruct(rim.shape, BF16),
+        ],
+        in_specs=[vmem] * 2,
+        out_specs=[vmem] * 5,
+        scratch_shapes=[
+            pltpu.VMEM((half, LANES), BF16),
+            pltpu.VMEM((lat_count - 1, part, LANES), BF16),
+            pltpu.VMEM((lon_count // 2 - 1, chunk, LANES), BF16),
+            pltpu.VMEM((half, LANES), BF16),
+            pltpu.VMEM((part, LANES), BF16),
+            pltpu.VMEM((total_rows, LANES), BF16),
+            pltpu.VMEM(rim.shape, BF16),
+            pltpu.VMEM((C, 4 * C), F32),
+            pltpu.SemaphoreType.DMA((copies,)),
+            pltpu.SemaphoreType.DMA((copies,)),
+        ],
+        compiler_params=pltpu.CompilerParams(
+            collective_id=0, has_side_effects=True, vmem_limit_bytes=48 * 2**20
+        ),
+        name="reduce_and_push",
+    )(totals, rim)
+    at = 0
+    got = []
+    for cut, source, n in zip(cuts, flat, lengths):
+        got.append(rim[at : at + source.shape[0]].reshape(cut.shape))
+        at += n
+    upper = jnp.concatenate([frame[:, rim_rows:, rim_cols:], got[0]], axis=2)
+    lower = jnp.concatenate([got[1], got[2]], axis=2)
+    owned = jnp.concatenate([upper, lower], axis=1)
     owned = jnp.where(row_mask, owned, jnp.zeros_like(owned))
     merged = merge_patches(owned[..., :feat_count], merge_weight)
-    return (merged, owned[..., feat_count:]) + tuple(summed)
+    return (merged, owned[..., feat_count:]) + tuple(grads)
 
 
 def solution(mesh):

time: 193 us -> 73.9 us (0.38)
  waiting for transfers between devices: 128 us -> 0.01 us
  Pallas kernels: 23.8 us -> 52.6 us
  between operations: 14.4 us -> 1.08 us
  local copies, waits for them, and re-layouts: 13.3 us -> 10.8 us
    psum x1 -> x0, waiting for transfers between devices: 117 us -> none  [per_device(): lax.psum((qkv_total, proj_total, up_total, down_total), ('lon', 'lat'))]
    pallas_call x0 -> x1, Pallas kernels: none -> 29.4 us  [per_device(): pl.pallas_call(functools.partial(reduce_kernel, lon_count, lat_count, len...]
    ppermute x4 -> x2, waiting for transfers between devices: 10.6 us -> 0.01 us  [shifted(): return lax.ppermute(block, axis, route)]
    ppermute x4 -> x2, starting transfers between devices: 7.92 us -> 6.63 us  [shifted(): return lax.ppermute(block, axis, route)]
    unnamed x40 -> x30, local copies, waits for them, and re-layouts: 8.57 us -> 8.62 us
  transfers between devices with their start and end apart: 5 -> 2, of which waited for: 3 -> 0; matrix products, arithmetic and copies ran while one was open for 2% -> 1% of each run, Pallas kernels for 9% -> 23%
where the time goes in v2:
time: 73.9 us; the launch traced here: 73.6 us
  Pallas kernels  52.6 us (71%)
  local copies, waits for them, and re-layouts  10.8 us (15%)
  starting transfers between devices  6.63 us (9%)
  other arithmetic  2.26 us (3%)
  between operations  1.08 us (1%)
    pallas_call x1, Pallas kernels, per_device(): pl.pallas_call(functools.partial(reduce_kernel, lon_count, lat_count, len...  29.4 us
    pallas_call x1, Pallas kernels, per_device(): pl.pallas_call(functools.partial(gather_kernel, pieces), out_shape=jax.Sh...  16.6 us
    unnamed x30, local copies, waits for them, and re-layouts  8.62 us
    pallas_call x1, Pallas kernels, per_device(): pl.pallas_call(functools.partial(block_kernel, window_rows), out_shape=[w...  6.65 us
    ppermute x2, starting transfers between devices, shifted(): return lax.ppermute(block, axis, route)  6.63 us
  transfers between devices with their start and end apart: 2, of which 0 were waited for; matrix products, arithmetic and copies ran while one was open for 1% of the time, Pallas kernels for 23%

profile of v2, /device:TPU:1, one launch (start us, length us, event | category | flops | bytes accessed | tf_op | source)
XLA Modules:
  0.0 73.6 jit_solution(8159937081345330588)
XLA Ops:
  0.7 1.0 %copy.48 = bf16[2,12,12,192]{3,2,1,0:T(8,128)(2,1)S(1)} copy(bf16[2,12,12,192]{3,0,2,1:T(2,128)(2,1)} %param.11) | data formatting | bytes 221184 | tf_op args[0]
  1.9 3.9 %collective-permute-start = (bf16[2,3,12,384]{3,2,1,0:T(8,128)(2,1)S(1)}, bf16[2,3,12,384]{3,2,1,0:T(8,128)(2,1)S(1)}, u32[]{:S(2)}, u32[]{:S(2)}) collective-permute-start(bf16[2,3,12,384]{3,2,1,0:T(8,128)(2,1)S(1)} %slice.68), channel_id=1, source_target_pairs={{0,1},{1,2},{2,3},{4,5},{5,6},{6,7},{8,9},{9,10},{10,11},{12,13},{... | collective-permute-start | bytes 165896 | tf_op jit(solution)/shard_map/ppermute | solution.py:34
  6.0 0.9 %copy-done.8 = s32[20736]{0:T(1024)S(1)} copy-done((s32[20736]{0:T(1024)S(1)}, s32[20736]{0:T(1024)}, u32[]{:S(2)}) %copy-start.8) | copy-done | bytes 82968
  6.9 0.3 reshape.123
  7.4 2.7 %collective-permute-start.1 = (bf16[2,12,6,384]{3,2,1,0:T(8,128)(2,1)S(1)}, bf16[2,12,6,384]{3,2,1,0:T(8,128)(2,1)}, u32[]{:S(2)}, u32[]{:S(2)}) collective-permute-start(bf16[2,12,6,384]{3,2,1,0:T(8,128)(2,1)S(1)} %fusion.7), channel_id=1, source_target_pairs={{0,4},{4,8},{8,12},{12,16},{16,20},{20,24},{24,28},{28,0},{1,5},{5... | collective-permute-start | bytes 331784 | tf_op jit(solution)/shard_map/ppermute | solution.py:34
  10.3 0.3 copy.53.down_ref
  10.6 16.6 %bias_gather.1.bias_ref = f32[12,144,128]{2,1,0:T(8,128)S(1)} custom-call(s32[144,128]{1,0:T(8,128)S(1)} %pad.20.index_ref, f32[12,26,128]{2,1,0:T(8,128)S(1)} %reshape.135.table_ref), custom_call_target="tpu_custom_call" | custom-call | flops 1000000000 | bytes 4000000 | tf_op jit(solution)/shard_map/bias_gather/pallas_call | solution.py:392
  27.2 1.0 %fusion.4 = bf16[2,12,12,384]{3,2,1,0:T(8,128)(2,1)S(1)} fusion(bf16[2,9,12,384]{3,2,1,0:T(8,128)(2,1)S(1)} %slice.69, bf16[2,3,12,384]{3,2,1,0:T(8,128)(2,1)S(1)} %collective-permute-done, bf16[2,12,6,384]{3,2,1,0:T(8,128)(2,1)} %collective-permute-done.1), kind=kLoop, calls=%fused_computation.10 | loop fusion | flops 663552 | bytes 552960 | tf_op jit(solution)/shard_map/concatenate | solution.py:41
  28.4 0.7 copy-done.3
  29.1 0.3 copy-done.1
  29.4 1.0 %copy-done.2 = s32[192,576]{1,0:T(8,128)S(1)} copy-done((s32[192,576]{1,0:T(8,128)S(1)}, s32[192,576]{1,0:T(8,128)}, u32[]{:S(2)}) %copy-start.2) | copy-done | bytes 442392
  30.4 6.7 %block.1 = (bf16[288,192]{1,0:T(8,128)(2,1)S(1)}, bf16[288,192]{1,0:T(8,128)(2,1)S(1)}, bf16[3584,128]{1,0:T(8,128)(2,1)S(1)}) custom-call(s32[4]{0:T(128)S(1)} %reshape.121.edges_ref, s32[4]{0:T(128)S(1)} %copy-done.4, s32[4]{0:T(128)S(1)} %copy-done.5, bf16[288,192]{1,0:T(8,128)(2,1)S(1)} %get-tuple-element.53.start_ref, ...), custom_call_target="tpu_custom_call" | custom-call | tf_op jit(solution)/shard_map/block/pallas_call | solution.py:408
  37.5 29.4 %reduce_and_push.1 = (bf16[192,576]{1,0:T(8,128)(2,1)S(1)}, bf16[192,192]{1,0:T(8,128)(2,1)S(1)}, bf16[192,768]{1,0:T(8,128)(2,1)S(1)}, bf16[768,192]{1,0:T(8,128)(2,1)S(1)}, bf16[208,384]{1,0:T(8,128)(2,1)S(1)}) custom-call(bf16[3584,128]{1,0:T(8,128)(2,1)S(1)} %get-tuple-element.16.totals_ref, bf16[208,384]{1,0:T(8,128)(2,1)S(1)} %fusion.6.rim_ref), custom_call_target="tpu_custom_call" | custom-call | tf_op jit(solution)/shard_map/reduce_and_push/pallas_call | solution.py:444
  67.2 0.2 copy.54
  67.5 0.2 reduce_sum.18
  67.8 0.3 multiply_reduce_fusion
  68.3 0.9 %copy.60 = bf16[768,192]{0,1:T(8,128)(2,1)} copy(bf16[768,192]{1,0:T(8,128)(2,1)S(1)} %get-tuple-element.45) | data formatting | bytes 589824
  69.1 0.8 %copy.59 = bf16[2,12,12,192]{3,0,2,1:T(2,128)(2,1)} copy(bf16[2,12,12,192]{3,2,1,0:T(8,128)(2,1)S(1)} %get-tuple-element.46) | data formatting | bytes 221184
  70.0 0.3 reshape.136
  70.6 0.3 convolution_convert_fusion
  70.9 0.7 copy.58
  71.6 0.7 copy.66
  72.2 0.6 copy.67
  72.9 0.7 copy.68
  (59 shorter events, 2.2 us)
Async XLA Ops:
  0.6 69.9 %copy-start = (bf16[768,384]{1,0:T(8,128)(2,1)S(1)}, bf16[768,384]{1,0:T(8,128)(2,1)}, u32[]{:S(2)}) copy-start(bf16[768,384]{1,0:T(8,128)(2,1)} %param.21) | copy-start | bytes 1769476
  0.7 1.0 %copy-start.7 = (bf16[2,12,12,192]{3,0,2,1:T(2,128)(2,1)S(1)}, bf16[2,12,12,192]{3,0,2,1:T(2,128)(2,1)}, u32[]{:S(2)}) copy-start(bf16[2,12,12,192]{3,0,2,1:T(2,128)(2,1)} %param.12) | copy-start | bytes 331780
  1.9 4.0 %copy-start.9 = (bf16[2,1,6,3312]{3,0,2,1:T(2,128)(2,1)S(1)}, bf16[2,1,6,3312]{3,0,2,1:T(2,128)(2,1)}, u32[]{:S(2)}) copy-start(bf16[2,1,6,3312]{3,0,2,1:T(2,128)(2,1)} %param.19) | copy-start | bytes 238468
  1.9 5.4 %collective-permute-start = (bf16[2,3,12,384]{3,2,1,0:T(8,128)(2,1)S(1)}, bf16[2,3,12,384]{3,2,1,0:T(8,128)(2,1)S(1)}, u32[]{:S(2)}, u32[]{:S(2)}) collective-permute-start(bf16[2,3,12,384]{3,2,1,0:T(8,128)(2,1)S(1)} %slice.68), channel_id=1, source_target_pairs={{0,1},{1,2},{2,3},{4,5},{5,6},{6,7},{8,9},{9,10},{10,11},{12,13},{... | collective-permute-start | bytes 165896 | tf_op jit(solution)/shard_map/ppermute | solution.py:34
  6.0 0.9 %copy-start.8 = (s32[20736]{0:T(1024)S(1)}, s32[20736]{0:T(1024)}, u32[]{:S(2)}) copy-start(s32[20736]{0:T(1024)} %param.20) | copy-start | bytes 248836
  7.3 3.0 %copy-start.6 = (s32[768,192]{0,1:T(8,128)S(1)}, s32[768,192]{0,1:T(8,128)}, u32[]{:S(2)}) copy-start(s32[768,192]{0,1:T(8,128)} %param.16) | copy-start | bytes 1769476
  7.4 19.8 %collective-permute-start.1 = (bf16[2,12,6,384]{3,2,1,0:T(8,128)(2,1)S(1)}, bf16[2,12,6,384]{3,2,1,0:T(8,128)(2,1)}, u32[]{:S(2)}, u32[]{:S(2)}) collective-permute-start(bf16[2,12,6,384]{3,2,1,0:T(8,128)(2,1)S(1)} %fusion.7), channel_id=1, source_target_pairs={{0,4},{4,8},{8,12},{12,16},{16,20},{20,24},{24,28},{28,0},{1,5},{5... | collective-permute-start | bytes 331784 | tf_op jit(solution)/shard_map/ppermute | solution.py:34
  28.2 0.9 %copy-start.3 = (s32[192,192]{1,0:T(8,128)S(1)}, s32[192,192]{1,0:T(8,128)}, u32[]{:S(2)}) copy-start(s32[192,192]{1,0:T(8,128)} %proj_ref.1) | copy-start | bytes 442372
  28.3 1.1 %copy-start.1 = (s32[192,768]{1,0:T(8,128)S(1)}, s32[192,768]{1,0:T(8,128)}, u32[]{:S(2)}) copy-start(s32[192,768]{1,0:T(8,128)} %up_ref.1) | copy-start | bytes 1769476
  28.4 1.0 %copy-start.4 = (s32[4]{0:T(128)S(1)}, s32[4]{0:T(128)}, u32[]{:S(2)}) copy-start(s32[4]{0:T(128)} %bits_ref.1) | copy-start | bytes 52
  28.4 1.0 %copy-start.5 = (s32[4]{0:T(128)S(1)}, s32[4]{0:T(128)}, u32[]{:S(2)}) copy-start(s32[4]{0:T(128)} %scales_ref.1) | copy-start | bytes 52
  29.4 1.0 %copy-start.2 = (s32[192,576]{1,0:T(8,128)S(1)}, s32[192,576]{1,0:T(8,128)}, u32[]{:S(2)}) copy-start(s32[192,576]{1,0:T(8,128)} %qkv_ref.1) | copy-start | bytes 1327108

commit v3 on v2

--- a/solution.py
+++ b/solution.py
@@ -18,6 +18,8 @@
 WTOK = 144
 HALF = 72
 LANES = 128
+PIECE = 256
+STEPS = 12
 EPSILON = 1e-05
 MASKED = -1000000000.0
 UP_AT = 6 * C
@@ -28,19 +30,6 @@
 BF16 = jnp.bfloat16
 
 
-def shifted(block, axis, by, wrap):
-    count = lax.axis_size(axis)
-    route = [(i, (i + by) % count) for i in range(count) if wrap or 0 <= i + by < count]
-    return lax.ppermute(block, axis, route)
-
-
-def pull_rim(source):
-    lat_part = shifted(source[:, -(WLAT // 2) :], "lat", 1, False)
-    upper = jnp.concatenate([lat_part, source[:, : -(WLAT // 2)]], axis=1)
-    lon_part = shifted(upper[:, :, -(WLON // 2) :], "lon", 1, True)
-    return jnp.concatenate([lon_part, upper[:, :, : -(WLON // 2)]], axis=2)
-
-
 def nn(left, right):
     return lax.dot_general(left, right, (((1,), (0,)), ((), ())), preferred_element_type=F32)
 
@@ -53,21 +42,79 @@
     return lax.dot_general(left, right, (((0,), (0,)), ((), ())), preferred_element_type=F32)
 
 
-def gather_kernel(pieces, index_ref, table_ref, out_ref):
-    index = index_ref[...]
-    low = jnp.bitwise_and(index, LANES - 1)
-    high = jnp.right_shift(index, 7)
-
-    def one_row(r, carry):
-        total = jnp.zeros(index.shape, F32)
-        for piece in range(pieces):
-            source = jnp.broadcast_to(table_ref[r, pl.ds(piece, 1), :], index.shape)
-            found = jnp.take_along_axis(source, low, axis=1, mode="promise_in_bounds")
-            total = jnp.where(high == piece, found, total)
-        out_ref[r] = total
+def neighbours(lon_count, lat_count):
+    lon, lat = lax.axis_index("lon"), lax.axis_index("lat")
+    west, east = lax.rem(lon + lon_count - 1, lon_count), lax.rem(lon + 1, lon_count)
+    north, south = lax.rem(lat + lat_count - 1, lat_count), lax.rem(lat + 1, lat_count)
+    behind = [{"lon": west, "lat": lat}, {"lon": lon, "lat": north}, {"lon": west, "lat": north}]
+    ahead = [{"lon": east, "lat": lat}, {"lon": lon, "lat": south}, {"lon": east, "lat": south}]
+    return behind, ahead
+
+
+def greet(devices):
+    barrier = pltpu.get_barrier_semaphore()
+    for device in devices:
+        pl.semaphore_signal(barrier, inc=1, device_id=device, device_id_type=pl.DeviceIdType.MESH)
+    pl.semaphore_wait(barrier, len(devices))
+
+
+def pull_kernel(
+    lon_count,
+    lat_count,
+    rim_parts,
+    rim_ref,
+    index_ref,
+    table_ref,
+    rim_out_ref,
+    bias_ref,
+    rim_in,
+    sends,
+    receives,
+):
+    behind, ahead = neighbours(lon_count, lat_count)
+    greet(behind + ahead)
+    copies = []
+    at = 0
+    for slot, (length, device) in enumerate(zip(rim_parts, ahead)):
+        copy = pltpu.make_async_remote_copy(
+            src_ref=rim_ref.at[pl.ds(at, length)],
+            dst_ref=rim_in.at[pl.ds(at, length)],
+            send_sem=sends.at[slot],
+            recv_sem=receives.at[slot],
+            device_id=device,
+            device_id_type=pl.DeviceIdType.MESH,
+        )
+        copy.start()
+        copies.append(copy)
+        at += length
+
+    steps, width = index_ref.shape
+    table_rows = bias_ref.shape[0]
+    pieces, piece_rows, piece = table_ref.shape
+    tables = table_ref[...].reshape(pieces * piece_rows, piece)
+    inside = lax.broadcasted_iota(jnp.int32, (piece, width), 0)
+
+    def one_step(step, carry):
+        index = index_ref[pl.ds(step, 1), :]
+        low = jnp.bitwise_and(index, piece - 1)
+        high = jnp.right_shift(index, piece.bit_length() - 1)
+        chosen = jnp.where(inside == low, 1.0, 0.0).astype(BF16)
+        found = nn(tables, chosen)
+        total = found[:piece_rows]
+        for p in range(1, pieces):
+            total = jnp.where(high == p, found[p * piece_rows : (p + 1) * piece_rows], total)
+        for i in range(width // LANES):
+            for r in range(table_rows):
+                row = total[r : r + 1, i * LANES : (i + 1) * LANES]
+                bias_ref[r, pl.ds(step * (width // LANES) + i, 1), :] = row
         return carry
 
-    lax.fori_loop(0, table_ref.shape[0], one_row, 0)
+    lax.fori_loop(0, steps, one_step, 0)
+    for copy in copies:
+        copy.wait_recv()
+    rim_out_ref[...] = rim_in[...]
+    for copy in copies:
+        copy.wait_send()
 
 
 def center_of(values):
@@ -246,24 +293,10 @@
         return {"lon": other * 2 + core, "lat": lat}
 
     twin = {"lon": far * 2 + 1 - core, "lat": lat}
-    west, east = lax.rem(lon + lon_count - 1, lon_count), lax.rem(lon + 1, lon_count)
-    north, south = lax.rem(lat + lat_count - 1, lat_count), lax.rem(lat + 1, lat_count)
-    rim_to = [
-        {"lon": west, "lat": lat},
-        {"lon": lon, "lat": north},
-        {"lon": west, "lat": north},
-    ]
-    rim_from = [
-        {"lon": east, "lat": lat},
-        {"lon": lon, "lat": south},
-        {"lon": east, "lat": south},
-    ]
+    rim_to, rim_from = neighbours(lon_count, lat_count)
     greeted = [twin] + [across(d) for d in range(1, lat_count)]
     greeted += [along(d) for d in range(1, far_count)] + rim_to + rim_from
-    barrier = pltpu.get_barrier_semaphore()
-    for device in greeted:
-        pl.semaphore_signal(barrier, inc=1, device_id=device, device_id_type=pl.DeviceIdType.MESH)
-    pl.semaphore_wait(barrier, len(greeted))
+    greet(greeted)
 
     used = []
 
@@ -350,6 +383,21 @@
     center, inverse = center_of(grouped.astype(F32))
     merged = nn((center * inverse).astype(BF16), merge_weight).astype(BF16)
     return merged.reshape(level_count, row_count // 2, col_count // 2, 2 * feat_count)
+
+
+def packed(cuts):
+    flat = [cut.reshape(-1, cut.shape[-1]) for cut in cuts]
+    lengths = [-(-cut.shape[0] // 16) * 16 for cut in flat]
+    padded = [jnp.pad(cut, ((0, n - cut.shape[0]), (0, 0))) for cut, n in zip(flat, lengths)]
+
+    def unpack(buffer):
+        starts = [sum(lengths[:i]) for i in range(len(cuts))]
+        return [
+            buffer[at : at + part.shape[0]].reshape(cut.shape)
+            for at, part, cut in zip(starts, flat, cuts)
+        ]
+
+    return jnp.concatenate(padded, axis=0), lengths, unpack
 
 
 def per_device(
@@ -377,32 +425,48 @@
 
     both = jnp.concatenate([tokens, cotangent], axis=-1)
     both = jnp.where(row_mask, both, jnp.zeros_like(both))
-    frame = pull_rim(both).reshape(token_count, 2 * feat_count)
-
+    lon_count, lat_count = lax.axis_size("lon"), lax.axis_size("lat")
+    rim_rows, rim_cols = WLAT // 2, WLON // 2
+    pulled, lengths, unpack = packed(
+        [both[:, :-rim_rows, rim_cols:], both[:, -rim_rows:, :rim_cols], both[:, -rim_rows:, rim_cols:]]
+    )
     pair = bias_index.reshape(2, HALF, 2, HALF)
     index = jnp.concatenate([pair[0, :, 0], pair[1, :, 1]], axis=0)
-    index = jnp.pad(index, ((0, 0), (0, LANES - HALF)))
+    index = jnp.pad(index, ((0, 0), (0, LANES - HALF))).reshape(STEPS, -1)
     positions = bias_table.shape[-1]
-    pieces = -(-positions // LANES)
-    table = bias_table.reshape(window_rows * HEADS, positions).astype(F32)
-    table = jnp.pad(table, ((0, 0), (0, pieces * LANES - positions)))
-    table = table.reshape(window_rows * HEADS, pieces, LANES)
+    table_rows = window_rows * HEADS
+    pieces, piece_rows = -(-positions // PIECE), -(-table_rows // 16) * 16
+    table = bias_table.reshape(table_rows, positions)
+    spare = ((0, piece_rows - table_rows), (0, pieces * PIECE - positions))
+    table = jnp.pad(table, spare).reshape(piece_rows, pieces, PIECE).transpose(1, 0, 2)
     vmem = pl.BlockSpec(memory_space=pltpu.VMEM)
     smem = pl.BlockSpec(memory_space=pltpu.SMEM)
-    bias = pl.pallas_call(
-        functools.partial(gather_kernel, pieces),
-        out_shape=jax.ShapeDtypeStruct((window_rows * HEADS, WTOK, LANES), F32),
-        in_specs=[vmem, vmem],
-        out_specs=vmem,
-        compiler_params=pltpu.CompilerParams(vmem_limit_bytes=32 * 2**20),
-        cost_estimate=pl.CostEstimate(flops=10**9, bytes_accessed=4 * 10**6, transcendentals=0),
-        name="bias_gather",
-    )(index, table)
+    pulled, bias = pl.pallas_call(
+        functools.partial(pull_kernel, lon_count, lat_count, lengths),
+        out_shape=[
+            jax.ShapeDtypeStruct(pulled.shape, BF16),
+            jax.ShapeDtypeStruct((table_rows, WTOK, LANES), F32),
+        ],
+        in_specs=[vmem] * 3,
+        out_specs=[vmem] * 2,
+        scratch_shapes=[
+            pltpu.VMEM(pulled.shape, BF16),
+            pltpu.SemaphoreType.DMA((len(lengths),)),
+            pltpu.SemaphoreType.DMA((len(lengths),)),
+        ],
+        compiler_params=pltpu.CompilerParams(
+            collective_id=1, has_side_effects=True, vmem_limit_bytes=32 * 2**20
+        ),
+        name="pull_and_bias",
+    )(pulled, index, table)
+    got = unpack(pulled)
+    upper = jnp.concatenate([got[2], got[1]], axis=2)
+    lower = jnp.concatenate([got[0], both[:, :-rim_rows, :rim_cols]], axis=2)
+    frame = jnp.concatenate([upper, lower], axis=1).reshape(token_count, 2 * feat_count)
 
     first_row = lat_start + WLAT * jnp.arange(window_rows, dtype=jnp.int32)
     edges = jnp.stack([-first_row * WLON, (lat_limit - first_row) * WLON], axis=1).reshape(-1)
     wide = jax.ShapeDtypeStruct((token_count, feat_count), BF16)
-    lon_count, lat_count = lax.axis_size("lon"), lax.axis_size("lat")
     chunk = -(-TOTAL_ROWS // (lon_count * lat_count * 16)) * 16
     total_rows = chunk * lon_count * lat_count
     final, grad, totals = pl.pallas_call(
@@ -427,18 +491,10 @@
         bias,
     )
     frame = jnp.concatenate([final, grad], axis=-1).reshape(grid_shape + (-1,))
-    rim_rows, rim_cols = WLAT // 2, WLON // 2
-    cuts = [
-        frame[:, rim_rows:, :rim_cols],
-        frame[:, :rim_rows, rim_cols:],
-        frame[:, :rim_rows, :rim_cols],
-    ]
-    flat = [cut.reshape(-1, 2 * feat_count) for cut in cuts]
-    lengths = [-(-cut.shape[0] // 16) * 16 for cut in flat]
-    rim = jnp.concatenate(
-        [jnp.pad(cut, ((0, n - cut.shape[0]), (0, 0))) for cut, n in zip(flat, lengths)], axis=0
+    rim, lengths, unpack = packed(
+        [frame[:, rim_rows:, :rim_cols], frame[:, :rim_rows, rim_cols:], frame[:, :rim_rows, :rim_cols]]
     )
-    copies = 2 * (1 + lat_count - 1 + lon_count // 2 - 1) + len(cuts)
+    copies = 2 * (1 + lat_count - 1 + lon_count // 2 - 1) + len(lengths)
     half = total_rows // 2
     part = half // lat_count
     *grads, rim = pl.pallas_call(
@@ -469,11 +525,7 @@
         ),
         name="reduce_and_push",
     )(totals, rim)
-    at = 0
-    got = []
-    for cut, source, n in zip(cuts, flat, lengths):
-        got.append(rim[at : at + source.shape[0]].reshape(cut.shape))
-        at += n
+    got = unpack(rim)
     upper = jnp.concatenate([frame[:, rim_rows:, rim_cols:], got[0]], axis=2)
     lower = jnp.concatenate([got[1], got[2]], axis=2)
     owned = jnp.concatenate([upper, lower], axis=1)

time: 73.9 us -> 61.2 us (0.83)
  Pallas kernels: 52.6 us -> 43.4 us
  starting transfers between devices: 6.63 us -> 0 us
  local copies, waits for them, and re-layouts: 10.8 us -> 14.8 us
  other arithmetic: 2.26 us -> 1.27 us
    pallas_call x1, Pallas kernels: 16.6 us -> 9.06 us  [per_device(): pl.pallas_call(functools.partial(pull_kernel, lon_count, lat_count, lengt...]
    ppermute x2 -> x0, starting transfers between devices: 6.63 us -> none  [shifted(): return lax.ppermute(block, axis, route)]
    unnamed x30, local copies, waits for them, and re-layouts: 8.62 us -> 12.5 us
    pallas_call x1, Pallas kernels: 29.4 us -> 27.6 us  [per_device(): pl.pallas_call(functools.partial(reduce_kernel, lon_count, lat_count, len...]
    concatenate x3, other arithmetic: 1.12 us -> 0.15 us  [the longest x1 0.1 us: per_device(): jnp.concatenate([upper, lower], axis=1).reshape(token_count, 2 * feat_count)]
  transfers between devices with their start and end apart: 2 -> 0, of which waited for: 0 -> 0; matrix products, arithmetic and copies ran while one was open for 1% -> 0% of each run, Pallas kernels for 23% -> 0%
where the time goes in v3:
time: 61.2 us; the launch traced here: 60.8 us
  Pallas kernels  43.4 us (71%)
  local copies, waits for them, and re-layouts  14.8 us (24%)
  other arithmetic  1.27 us (2%)
  between operations  1.07 us (2%)
    pallas_call x1, Pallas kernels, per_device(): pl.pallas_call(functools.partial(reduce_kernel, lon_count, lat_count, len...  27.6 us
    unnamed x30, local copies, waits for them, and re-layouts  12.5 us
    pallas_call x1, Pallas kernels, per_device(): pl.pallas_call(functools.partial(pull_kernel, lon_count, lat_count, lengt...  9.06 us
    pallas_call x1, Pallas kernels, per_device(): pl.pallas_call(functools.partial(block_kernel, window_rows), out_shape=[w...  6.65 us

profile of v3, /device:TPU:1, one launch (start us, length us, event | category | flops | bytes accessed | tf_op | source)
XLA Modules:
  0.0 60.8 jit_solution(13509183750311627613)
XLA Ops:
  0.8 0.9 %copy.57 = bf16[2,1,6,3312]{3,2,0,1:T(8,128)(2,1)S(1)} copy(bf16[2,1,6,3312]{3,0,2,1:T(2,128)(2,1)} %param.19) | data formatting | bytes 158976 | tf_op args[8]
  1.9 0.9 %copy-done.9 = s32[20736]{0:T(1024)S(1)} copy-done((s32[20736]{0:T(1024)S(1)}, s32[20736]{0:T(1024)}, u32[]{:S(2)}) %copy-start.9) | copy-done | bytes 82968
  2.7 0.3 reshape.144
  3.2 0.9 %copy-done.7 = bf16[2,12,12,192]{3,0,2,1:T(2,128)(2,1)S(1)} copy-done((bf16[2,12,12,192]{3,0,2,1:T(2,128)(2,1)S(1)}, bf16[2,12,12,192]{3,0,2,1:T(2,128)(2,1)}, u32[]{:S(2)}) %copy-start.7) | copy-done | bytes 110616
  4.1 0.9 %copy-done.8 = bf16[2,12,12,192]{3,0,2,1:T(2,128)(2,1)S(1)} copy-done((bf16[2,12,12,192]{3,0,2,1:T(2,128)(2,1)S(1)}, bf16[2,12,12,192]{3,0,2,1:T(2,128)(2,1)}, u32[]{:S(2)}) %copy-start.8) | copy-done | bytes 110616
  5.3 9.1 %pull_and_bias.1 = (bf16[208,384]{1,0:T(8,128)(2,1)S(1)}, f32[12,144,128]{2,1,0:T(8,128)S(1)}) custom-call(bf16[208,384]{1,0:T(8,128)(2,1)S(1)} %fusion.8.rim_ref, s32[12,1536]{1,0:T(8,128)S(1)} %reshape.145.index_ref, bf16[13,16,256]{2,1,0:T(8,128)(2,1)S(1)} %bitcast.17), custom_call_target="tpu_custom_call" | custom-call | tf_op jit(solution)/shard_map/pull_and_bias/pallas_call | solution.py:444
  14.8 0.9 %copy-done.6 = s32[768,192]{0,1:T(8,128)S(1)} copy-done((s32[768,192]{0,1:T(8,128)S(1)}, s32[768,192]{0,1:T(8,128)}, u32[]{:S(2)}) %copy-start.6) | copy-done | bytes 589848
  15.7 0.3 copy.59.down_ref
  15.9 0.4 copy-done.4
  16.3 1.1 %copy-done.1 = s32[192,768]{1,0:T(8,128)S(1)} copy-done((s32[192,768]{1,0:T(8,128)S(1)}, s32[192,768]{1,0:T(8,128)}, u32[]{:S(2)}) %copy-start.1) | copy-done | bytes 589848
  17.4 1.0 %copy-done.2 = s32[192,576]{1,0:T(8,128)S(1)} copy-done((s32[192,576]{1,0:T(8,128)S(1)}, s32[192,576]{1,0:T(8,128)}, u32[]{:S(2)}) %copy-start.2) | copy-done | bytes 442392
  18.4 0.9 %copy-done.3 = s32[192,192]{1,0:T(8,128)S(1)} copy-done((s32[192,192]{1,0:T(8,128)S(1)}, s32[192,192]{1,0:T(8,128)}, u32[]{:S(2)}) %copy-start.3) | copy-done | bytes 147480
  19.4 6.6 %block.1 = (bf16[288,192]{1,0:T(8,128)(2,1)S(1)}, bf16[288,192]{1,0:T(8,128)(2,1)S(1)}, bf16[3584,128]{1,0:T(8,128)(2,1)S(1)}) custom-call(s32[4]{0:T(128)S(1)} %reshape.140.edges_ref, s32[4]{0:T(128)S(1)} %copy-done.4, s32[4]{0:T(128)S(1)} %copy-done.5, bf16[288,192]{1,0:T(8,128)(2,1)S(1)} %get-tuple-element.61.start_ref, ...), custom_call_target="tpu_custom_call" | custom-call | tf_op jit(solution)/shard_map/block/pallas_call | solution.py:472
  26.4 27.6 %reduce_and_push.1 = (bf16[192,576]{1,0:T(8,128)(2,1)S(1)}, bf16[192,192]{1,0:T(8,128)(2,1)S(1)}, bf16[192,768]{1,0:T(8,128)(2,1)S(1)}, bf16[768,192]{1,0:T(8,128)(2,1)S(1)}, bf16[208,384]{1,0:T(8,128)(2,1)S(1)}) custom-call(bf16[3584,128]{1,0:T(8,128)(2,1)S(1)} %get-tuple-element.20.totals_ref, bf16[208,384]{1,0:T(8,128)(2,1)S(1)} %fusion.10.rim_ref), custom_call_target="tpu_custom_call" | custom-call | tf_op jit(solution)/shard_map/reduce_and_push/pallas_call | solution.py:500
  54.3 0.9 %copy.66 = bf16[768,192]{0,1:T(8,128)(2,1)} copy(bf16[768,192]{1,0:T(8,128)(2,1)S(1)} %get-tuple-element.49) | data formatting | bytes 589824
  55.3 0.8 %copy.65 = bf16[2,12,12,192]{3,0,2,1:T(2,128)(2,1)} copy(bf16[2,12,12,192]{3,2,1,0:T(8,128)(2,1)S(1)} %get-tuple-element.50) | data formatting | bytes 221184
  56.1 0.2 copy.60
  56.8 0.3 multiply_reduce_fusion
  57.2 0.3 reshape.160
  57.8 0.3 convolution_convert_fusion
  58.1 0.7 %copy.64 = bf16[2,6,6,384]{3,0,2,1:T(2,128)(2,1)} copy(bf16[2,6,6,384]{3,2,1,0:T(8,128)(2,1)S(1)} %reshape.159) | data formatting | bytes 110592
  58.7 0.7 %copy.74 = bf16[192,576]{1,0:T(8,128)(2,1)} copy(bf16[192,576]{1,0:T(8,128)(2,1)S(1)} %get-tuple-element.78) | data formatting | bytes 442368
  59.4 0.6 %copy.75 = bf16[192,192]{1,0:T(8,128)(2,1)} copy(bf16[192,192]{1,0:T(8,128)(2,1)S(1)} %get-tuple-element.79) | data formatting | bytes 147456
  60.1 0.7 %copy.76 = bf16[192,768]{1,0:T(8,128)(2,1)} copy(bf16[192,768]{1,0:T(8,128)(2,1)S(1)} %get-tuple-element.80) | data formatting | bytes 589824
  (64 shorter events, 2.5 us)
Async XLA Ops:
  0.6 57.1 %copy-start = (bf16[768,384]{1,0:T(8,128)(2,1)S(1)}, bf16[768,384]{1,0:T(8,128)(2,1)}, u32[]{:S(2)}) copy-start(bf16[768,384]{1,0:T(8,128)(2,1)} %param.21) | copy-start | bytes 1769476
  1.8 0.9 %copy-start.9 = (s32[20736]{0:T(1024)S(1)}, s32[20736]{0:T(1024)}, u32[]{:S(2)}) copy-start(s32[20736]{0:T(1024)} %param.20) | copy-start | bytes 248836
  3.1 0.9 %copy-start.7 = (bf16[2,12,12,192]{3,0,2,1:T(2,128)(2,1)S(1)}, bf16[2,12,12,192]{3,0,2,1:T(2,128)(2,1)}, u32[]{:S(2)}) copy-start(bf16[2,12,12,192]{3,0,2,1:T(2,128)(2,1)} %param.11) | copy-start | bytes 331780
  4.0 0.9 %copy-start.8 = (bf16[2,12,12,192]{3,0,2,1:T(2,128)(2,1)S(1)}, bf16[2,12,12,192]{3,0,2,1:T(2,128)(2,1)}, u32[]{:S(2)}) copy-start(bf16[2,12,12,192]{3,0,2,1:T(2,128)(2,1)} %param.12) | copy-start | bytes 331780
  14.6 1.1 %copy-start.6 = (s32[768,192]{0,1:T(8,128)S(1)}, s32[768,192]{0,1:T(8,128)}, u32[]{:S(2)}) copy-start(s32[768,192]{0,1:T(8,128)} %param.16) | copy-start | bytes 1769476
  15.7 0.7 %copy-start.4 = (s32[4]{0:T(128)S(1)}, s32[4]{0:T(128)}, u32[]{:S(2)}) copy-start(s32[4]{0:T(128)} %bits_ref.1) | copy-start | bytes 52
  15.7 0.7 %copy-start.5 = (s32[4]{0:T(128)S(1)}, s32[4]{0:T(128)}, u32[]{:S(2)}) copy-start(s32[4]{0:T(128)} %scales_ref.1) | copy-start | bytes 52
  16.3 1.1 %copy-start.1 = (s32[192,768]{1,0:T(8,128)S(1)}, s32[192,768]{1,0:T(8,128)}, u32[]{:S(2)}) copy-start(s32[192,768]{1,0:T(8,128)} %up_ref.1) | copy-start | bytes 1769476
  17.4 1.0 %copy-start.2 = (s32[192,576]{1,0:T(8,128)S(1)}, s32[192,576]{1,0:T(8,128)}, u32[]{:S(2)}) copy-start(s32[192,576]{1,0:T(8,128)} %qkv_ref.1) | copy-start | bytes 1327108
  18.4 0.9 %copy-start.3 = (s32[192,192]{1,0:T(8,128)S(1)}, s32[192,192]{1,0:T(8,128)}, u32[]{:S(2)}) copy-start(s32[192,192]{1,0:T(8,128)} %proj_ref.1) | copy-start | bytes 442372

commit v4 on v3

--- a/solution.py
+++ b/solution.py
@@ -24,7 +24,6 @@
 MASKED = -1000000000.0
 UP_AT = 6 * C
 DOWN_AT = 12 * C
-PAIR_AT = 16 * C
 TOTAL_ROWS = 18 * C
 F32 = jnp.float32
 BF16 = jnp.bfloat16
@@ -65,12 +64,26 @@
     rim_ref,
     index_ref,
     table_ref,
+    qkv_far,
+    proj_far,
+    up_far,
+    down_far,
     rim_out_ref,
     bias_ref,
+    qkv_ref,
+    proj_ref,
+    up_ref,
+    down_ref,
     rim_in,
     sends,
     receives,
+    fetches,
 ):
+    pairs = [(qkv_far, qkv_ref), (proj_far, proj_ref), (up_far, up_ref), (down_far, down_ref)]
+    fetched = []
+    for slot, (source, target) in enumerate(pairs):
+        fetched.append(pltpu.make_async_copy(source, target, fetches.at[slot]))
+        fetched[-1].start()
     behind, ahead = neighbours(lon_count, lat_count)
     greet(behind + ahead)
     copies = []
@@ -110,6 +123,8 @@
         return carry
 
     lax.fori_loop(0, steps, one_step, 0)
+    for copy in fetched:
+        copy.wait()
     for copy in copies:
         copy.wait_recv()
     rim_out_ref[...] = rim_in[...]
@@ -131,9 +146,7 @@
 
 def block_kernel(
     window_rows,
-    edges_ref,
-    bits_ref,
-    scales_ref,
+    scalars_ref,
     start_ref,
     d_out_ref,
     qkv_ref,
@@ -149,11 +162,10 @@
     dk_s,
     dv_s,
     narrow_s,
-    pair_s,
 ):
     def dequant(codes, layer, fan_in):
-        largest = jnp.left_shift(jnp.int32(1), bits_ref[layer] - 1) - 1
-        scale = jnp.full((1, codes.shape[1]), scales_ref[layer].astype(F32), F32)
+        largest = jnp.left_shift(jnp.int32(1), scalars_ref[layer] - 1) - 1
+        scale = jnp.full((1, codes.shape[1]), scalars_ref[4 + layer].astype(F32), F32)
         factor = math.sqrt(C / fan_in) / scale
         return (jnp.clip(codes, -largest, largest).astype(F32) * factor).astype(BF16)
 
@@ -191,7 +203,7 @@
         bias = bias_ref[a * HEADS : (a + 1) * HEADS, (1 - level) * HALF : (2 - level) * HALF, :]
         bias = bias.reshape(HEADS * HALF, LANES)[:, :HALF]
         scores = nt(stacked_q, k[part]) * HEAD_DIM ** (-0.5) + bias
-        allowed = (keys >= edges_ref[2 * a]) & (keys < edges_ref[2 * a + 1])
+        allowed = (keys >= scalars_ref[8 + 2 * a]) & (keys < scalars_ref[9 + 2 * a])
         scores = jnp.where(allowed, scores, MASKED)
         weights = jnp.exp(scores - jnp.max(scores, axis=-1, keepdims=True))
         weights = weights / jnp.sum(weights, axis=-1, keepdims=True)
@@ -203,20 +215,19 @@
     center_two, inverse_two = center_of(resid.astype(F32))
     normed_two = (center_two * inverse_two).astype(BF16)
     w_up = dequant(up_ref[...], 2, C)
-    w_down = dequant(down_ref[...], 3, FF)
+    w_down_t = dequant(down_ref[...], 3, FF)
     pre = nn(normed_two, w_up)
     cubic = math.sqrt(2 / math.pi)
     square = pre * pre
     bent = jnp.tanh(cubic * (pre + 0.044715 * square * pre))
     hidden = (0.5 * pre * (1.0 + bent)).astype(BF16)
-    final_ref[...] = (resid.astype(F32) + nn(hidden, w_down)).astype(BF16)
+    final_ref[...] = (resid.astype(F32) + nt(hidden, w_down_t)).astype(BF16)
     d_out = d_out_ref[...]
-    down_total = tn(hidden, d_out)
-    totals_ref[DOWN_AT : DOWN_AT + FF, :] = down_total[:, :LANES].astype(BF16)
-    pair_s[:, : C - LANES] = down_total[: FF // 2, LANES:]
-    pair_s[:, C - LANES :] = down_total[FF // 2 :, LANES:]
-    totals_ref[PAIR_AT : PAIR_AT + FF // 2, :] = pair_s[...].astype(BF16)
-    d_hidden = nt(d_out, w_down).astype(BF16).astype(F32)
+    down_total = tn(d_out, hidden).astype(BF16)
+    for t in range(FF // LANES):
+        rows = slice(DOWN_AT + t * C, DOWN_AT + (t + 1) * C)
+        totals_ref[rows, :] = down_total[:, t * LANES : (t + 1) * LANES]
+    d_hidden = nn(d_out, w_down_t).astype(BF16).astype(F32)
     slope = 0.5 * (1.0 + bent) + 0.5 * pre * (1.0 - bent * bent) * cubic * (
         1.0 + 3 * 0.044715 * square
     )
@@ -261,6 +272,7 @@
     lon_count,
     lat_count,
     rim_parts,
+    chunks,
     totals_ref,
     rim_ref,
     grad_qkv_ref,
@@ -281,10 +293,6 @@
 ):
     lon, lat = lax.axis_index("lon"), lax.axis_index("lat")
     core, far, far_count = lax.rem(lon, 2), lon // 2, lon_count // 2
-    half = result.shape[0] // 2
-    part = half // lat_count
-    chunk = part // far_count
-
     def across(distance):
         return {"lon": lon, "lat": lax.rem(lat + distance + lat_count, lat_count)}
 
@@ -314,53 +322,74 @@
         used.append(copy)
         return copy
 
-    def rows(index, size):
-        return pl.ds(pl.multiple_of(index * size, 16), size)
-
-    first = send(totals_ref.at[rows(1 - core, half)], core_in, twin)
+    def sum_piece(before, chunk):
+        part = chunk * far_count
+        half = part * lat_count
+        part_at, half_at, whole_at = before * far_count, before * far_count * lat_count, 0
+        whole_at = 2 * half_at
+
+        def rows(start, index, size):
+            return pl.ds(pl.multiple_of(start + index * size, 16), size)
+
+        arriving = core_in.at[pl.ds(half_at, half)]
+        first = send(totals_ref.at[rows(whole_at, 1 - core, half)], arriving, twin)
+        yield
+        first.wait_recv()
+        total = totals_ref[rows(whole_at, core, half), :].astype(F32)
+        total = total + core_in[pl.ds(half_at, half), :].astype(F32)
+        half_s[pl.ds(half_at, half), :] = total.astype(BF16)
+        copies = []
+        for d in range(1, lat_count):
+            source = half_s.at[rows(half_at, lax.rem(lat + d, lat_count), part)]
+            copies.append(send(source, lat_in.at[d - 1, pl.ds(part_at, part)], across(d)))
+        yield
+        total = half_s[rows(half_at, lat, part), :].astype(F32)
+        for d, copy in enumerate(copies):
+            copy.wait_recv()
+            total = total + lat_in[d, pl.ds(part_at, part), :].astype(F32)
+        part_s[pl.ds(part_at, part), :] = total.astype(BF16)
+        copies = []
+        for d in range(1, far_count):
+            source = part_s.at[rows(part_at, lax.rem(far + d, far_count), chunk)]
+            copies.append(send(source, far_in.at[d - 1, pl.ds(before, chunk)], along(d)))
+        yield
+        total = part_s[rows(part_at, far, chunk), :].astype(F32)
+        for d, copy in enumerate(copies):
+            copy.wait_recv()
+            total = total + far_in[d, pl.ds(before, chunk), :].astype(F32)
+        mine = rows(whole_at, (core * lat_count + lat) * far_count + far, chunk)
+        result[mine, :] = total.astype(BF16)
+        copies = [send(result.at[mine], result.at[mine], along(d)) for d in range(1, far_count)]
+        yield
+        for copy in copies:
+            copy.wait_recv()
+        mine = rows(whole_at, core * lat_count + lat, part)
+        copies = [send(result.at[mine], result.at[mine], across(d)) for d in range(1, lat_count)]
+        yield
+        for copy in copies:
+            copy.wait_recv()
+        mine = rows(whole_at, core, half)
+        last = send(result.at[mine], result.at[mine], twin)
+        yield
+        last.wait_recv()
+
+    pieces = [sum_piece(sum(chunks[:p]), chunk) for p, chunk in enumerate(chunks)]
+    for piece in pieces:
+        next(piece)
     rims = []
     at = 0
     for length, device in zip(rim_parts, rim_to):
         window = pl.ds(at, length)
         rims.append(send(rim_ref.at[window], rim_in.at[window], device))
         at += length
-    first.wait_recv()
-    half_s[...] = (totals_ref[rows(core, half), :].astype(F32) + core_in[...].astype(F32)).astype(BF16)
-
-    copies = []
-    for d in range(1, lat_count):
-        target = lax.rem(lat + d, lat_count)
-        copies.append(send(half_s.at[rows(target, part)], lat_in.at[d - 1], across(d)))
-    total = half_s[rows(lat, part), :].astype(F32)
-    for d, copy in enumerate(copies):
-        copy.wait_recv()
-        total = total + lat_in[d].astype(F32)
-    part_s[...] = total.astype(BF16)
-
-    copies = []
-    for d in range(1, far_count):
-        target = lax.rem(far + d, far_count)
-        copies.append(send(part_s.at[rows(target, chunk)], far_in.at[d - 1], along(d)))
-    total = part_s[rows(far, chunk), :].astype(F32)
-    for d, copy in enumerate(copies):
-        copy.wait_recv()
-        total = total + far_in[d].astype(F32)
-    mine = rows((core * lat_count + lat) * far_count + far, chunk)
-    result[mine, :] = total.astype(BF16)
-
-    copies = [send(result.at[mine], result.at[mine], along(d)) for d in range(1, far_count)]
-    for copy in copies:
-        copy.wait_recv()
-    mine = rows(core * lat_count + lat, part)
-    copies = [send(result.at[mine], result.at[mine], across(d)) for d in range(1, lat_count)]
-    for copy in copies:
-        copy.wait_recv()
-    mine = rows(core, half)
-    last = send(result.at[mine], result.at[mine], twin)
+    for _ in range(5):
+        for piece in pieces:
+            next(piece)
     for copy in rims:
         copy.wait_recv()
     rim_out_ref[...] = rim_in[...]
-    last.wait_recv()
+    for piece in pieces:
+        next(piece, None)
 
     for t in range(4 * C // LANES):
         narrow_s[:, t * LANES : (t + 1) * LANES] = result[t * C : (t + 1) * C, :].astype(F32)
@@ -368,10 +397,9 @@
     grad_proj_ref[...] = narrow_s[:, 3 * C :].astype(BF16)
     for t in range(FF // LANES):
         grad_up_ref[:, t * LANES : (t + 1) * LANES] = result[UP_AT + t * C : UP_AT + (t + 1) * C, :]
-    grad_down_ref[:, :LANES] = result[DOWN_AT : DOWN_AT + FF, :]
-    pair = result[PAIR_AT : PAIR_AT + FF // 2, :].astype(F32)
-    grad_down_ref[: FF // 2, LANES:] = pair[:, : C - LANES].astype(BF16)
-    grad_down_ref[FF // 2 :, LANES:] = pair[:, C - LANES :].astype(BF16)
+    for t in range(FF // LANES):
+        rows = slice(DOWN_AT + t * C, DOWN_AT + (t + 1) * C)
+        grad_down_ref[:, t * LANES : (t + 1) * LANES] = result[rows, :]
     for copy in used:
         copy.wait_send()
 
@@ -441,24 +469,27 @@
     table = jnp.pad(table, spare).reshape(piece_rows, pieces, PIECE).transpose(1, 0, 2)
     vmem = pl.BlockSpec(memory_space=pltpu.VMEM)
     smem = pl.BlockSpec(memory_space=pltpu.SMEM)
-    pulled, bias = pl.pallas_call(
+    codes = (qkv_codes, proj_codes, up_codes, down_codes.T)
+    pulled, bias, *codes = pl.pallas_call(
         functools.partial(pull_kernel, lon_count, lat_count, lengths),
         out_shape=[
             jax.ShapeDtypeStruct(pulled.shape, BF16),
             jax.ShapeDtypeStruct((table_rows, WTOK, LANES), F32),
-        ],
-        in_specs=[vmem] * 3,
-        out_specs=[vmem] * 2,
+        ]
+        + [jax.ShapeDtypeStruct(code.shape, jnp.int32) for code in codes],
+        in_specs=[vmem] * 3 + [pl.BlockSpec(memory_space=pl.ANY)] * 4,
+        out_specs=[vmem] * 6,
         scratch_shapes=[
             pltpu.VMEM(pulled.shape, BF16),
             pltpu.SemaphoreType.DMA((len(lengths),)),
             pltpu.SemaphoreType.DMA((len(lengths),)),
+            pltpu.SemaphoreType.DMA((len(codes),)),
         ],
         compiler_params=pltpu.CompilerParams(
-            collective_id=1, has_side_effects=True, vmem_limit_bytes=32 * 2**20
+            collective_id=1, has_side_effects=True, vmem_limit_bytes=48 * 2**20
         ),
         name="pull_and_bias",
-    )(pulled, index, table)
+    )(pulled, index, table, *codes)
     got = unpack(pulled)
     upper = jnp.concatenate([got[2], got[1]], axis=2)
     lower = jnp.concatenate([got[0], both[:, :-rim_rows, :rim_cols]], axis=2)
@@ -472,38 +503,35 @@
     final, grad, totals = pl.pallas_call(
         functools.partial(block_kernel, window_rows),
         out_shape=[wide, wide, jax.ShapeDtypeStruct((total_rows, LANES), BF16)],
-        in_specs=[smem] * 3 + [vmem] * 7,
+        in_specs=[smem] + [vmem] * 7,
         out_specs=[vmem] * 3,
         scratch_shapes=[pltpu.VMEM((token_count, feat_count), F32)] * 4
-        + [pltpu.VMEM((C, 4 * C), F32), pltpu.VMEM((FF // 2, LANES), F32)],
+        + [pltpu.VMEM((C, 4 * C), F32)],
         compiler_params=pltpu.CompilerParams(vmem_limit_bytes=48 * 2**20),
         name="block",
     )(
-        edges,
-        bit_widths,
-        quant_scales,
+        jnp.concatenate([bit_widths, quant_scales, edges]),
         frame[:, :feat_count],
         frame[:, feat_count:],
-        qkv_codes,
-        proj_codes,
-        up_codes,
-        down_codes,
+        *codes,
         bias,
     )
     frame = jnp.concatenate([final, grad], axis=-1).reshape(grid_shape + (-1,))
     rim, lengths, unpack = packed(
         [frame[:, rim_rows:, :rim_cols], frame[:, :rim_rows, rim_cols:], frame[:, :rim_rows, :rim_cols]]
     )
-    copies = 2 * (1 + lat_count - 1 + lon_count // 2 - 1) + len(lengths)
+    units = chunk // 16
+    chunks = [16 * n for n in (units - units // 2, units // 2) if n]
+    copies = 2 * (1 + lat_count - 1 + lon_count // 2 - 1) * len(chunks) + len(lengths)
     half = total_rows // 2
     part = half // lat_count
     *grads, rim = pl.pallas_call(
-        functools.partial(reduce_kernel, lon_count, lat_count, lengths),
+        functools.partial(reduce_kernel, lon_count, lat_count, lengths, chunks),
         out_shape=[
             jax.ShapeDtypeStruct((C, 3 * C), BF16),
             jax.ShapeDtypeStruct((C, C), BF16),
             jax.ShapeDtypeStruct((C, FF), BF16),
-            jax.ShapeDtypeStruct((FF, C), BF16),
+            jax.ShapeDtypeStruct((C, FF), BF16),
             jax.ShapeDtypeStruct(rim.shape, BF16),
         ],
         in_specs=[vmem] * 2,
@@ -531,7 +559,7 @@
     owned = jnp.concatenate([upper, lower], axis=1)
     owned = jnp.where(row_mask, owned, jnp.zeros_like(owned))
     merged = merge_patches(owned[..., :feat_count], merge_weight)
-    return (merged, owned[..., feat_count:]) + tuple(grads)
+    return (merged, owned[..., feat_count:]) + tuple(grads[:3]) + (grads[3].T,)
 
 
 def solution(mesh):

time: 61.2 us -> 63.6 us (1.039)
  local copies, waits for them, and re-layouts: 14.8 us -> 18.6 us
  Pallas kernels: 43.4 us -> 41.8 us
    unnamed x30 -> x39, local copies, waits for them, and re-layouts: 12.5 us -> 15.7 us
    pallas_call x1, Pallas kernels: 27.6 us -> 25.4 us  [per_device(): pl.pallas_call(functools.partial(reduce_kernel, lon_count, lat_count, len...]
    pallas_call x1, Pallas kernels: 9.06 us -> 9.87 us  [per_device(): pl.pallas_call(functools.partial(pull_kernel, lon_count, lat_count, lengt...]
where the time goes in v4:
time: 63.6 us; the launch traced here: 63.1 us
  Pallas kernels  41.8 us (66%)
  local copies, waits for them, and re-layouts  18.6 us (29%)
  other arithmetic  1.34 us (2%)
  between operations  1.06 us (2%)
    pallas_call x1, Pallas kernels, per_device(): pl.pallas_call(functools.partial(reduce_kernel, lon_count, lat_count, len...  25.4 us
    unnamed x39, local copies, waits for them, and re-layouts  15.7 us
    pallas_call x1, Pallas kernels, per_device(): pl.pallas_call(functools.partial(pull_kernel, lon_count, lat_count, lengt...  9.87 us
    pallas_call x1, Pallas kernels, per_device(): pl.pallas_call(functools.partial(block_kernel, window_rows), out_shape=[w...  6.53 us

profile of v4, /device:TPU:1, one launch (start us, length us, event | category | flops | bytes accessed | tf_op | source)
XLA Modules:
  0.0 63.1 jit_solution(11208288269776986430)
XLA Ops:
  0.8 0.6 copy-done.13
  1.6 0.9 %copy.51 = bf16[2,1,6,3312]{3,2,0,1:T(8,128)(2,1)S(1)} copy(bf16[2,1,6,3312]{3,0,2,1:T(2,128)(2,1)} %param.19) | data formatting | bytes 158976 | tf_op args[8]
  2.6 0.9 %copy-done.12 = s32[20736]{0:T(1024)S(1)} copy-done((s32[20736]{0:T(1024)S(1)}, s32[20736]{0:T(1024)}, u32[]{:S(2)}) %copy-start.12) | copy-done | bytes 82968
  3.9 0.9 %copy-done.10 = bf16[2,12,12,192]{3,0,2,1:T(2,128)(2,1)S(1)} copy-done((bf16[2,12,12,192]{3,0,2,1:T(2,128)(2,1)S(1)}, bf16[2,12,12,192]{3,0,2,1:T(2,128)(2,1)}, u32[]{:S(2)}) %copy-start.10) | copy-done | bytes 110616
  4.8 0.9 %copy-done.11 = bf16[2,12,12,192]{3,0,2,1:T(2,128)(2,1)S(1)} copy-done((bf16[2,12,12,192]{3,0,2,1:T(2,128)(2,1)S(1)}, bf16[2,12,12,192]{3,0,2,1:T(2,128)(2,1)}, u32[]{:S(2)}) %copy-start.11) | copy-done | bytes 110616
  5.9 0.7 %fusion.16 = (bf16[2,9,6,384]{3,2,1,0:T(8,128)(2,1)S(1)}, bf16[2,9,6,384]{3,2,1,0:T(8,128)(2,1)}) fusion(bf16[2,12,12,384]{3,2,1,0:T(8,128)(2,1)S(1)} %maximum_select_fusion), kind=kLoop, calls=%fused_computation.38 | loop fusion | bytes 331776 | tf_op jit(solution)/shard_map/slice | solution.py:459
  7.0 0.6 %copy-done.6 = s32[192,192]{1,0:T(8,128)S(1)} copy-done((s32[192,192]{1,0:T(8,128)S(1)}, s32[192,192]{1,0:T(8,128)}, u32[]{:S(2)}) %copy-start.6) | copy-done | bytes 147480
  7.6 1.1 %copy-done.4 = s32[768,192]{0,1:T(8,128)S(1)} copy-done((s32[768,192]{0,1:T(8,128)S(1)}, s32[768,192]{0,1:T(8,128)}, u32[]{:S(2)}) %copy-start.4) | copy-done | bytes 589848
  8.7 1.0 %copy-done.5 = s32[192,576]{1,0:T(8,128)S(1)} copy-done((s32[192,576]{1,0:T(8,128)S(1)}, s32[192,576]{1,0:T(8,128)}, u32[]{:S(2)}) %copy-start.5) | copy-done | bytes 442392
  9.7 9.9 %pull_and_bias.1 = (bf16[208,384]{1,0:T(8,128)(2,1)S(1)}, f32[12,144,128]{2,1,0:T(8,128)S(1)}, s32[192,576]{1,0:T(8,128)S(1)}, s32[192,192]{1,0:T(8,128)S(1)}, s...) custom-call(bf16[208,384]{1,0:T(8,128)(2,1)S(1)} %fusion.8.rim_ref, s32[12,1536]{1,0:T(8,128)S(1)} %reshape.145.index_ref, ...), custom_call_target="tpu_custom_call" | custom-call | tf_op jit(solution)/shard_map/pull_and_bias/pallas_call | solution.py:473
  19.6 0.8 %copy-done.1 = s32[192,768]{1,0:T(8,128)} copy-done((s32[192,768]{1,0:T(8,128)}, s32[192,768]{1,0:T(8,128)S(1)}, u32[]{:S(2)}) %copy-start.1) | copy-done | bytes 589848
  20.4 0.7 %copy-done.7 = s32[192,192]{1,0:T(8,128)} copy-done((s32[192,192]{1,0:T(8,128)}, s32[192,192]{1,0:T(8,128)S(1)}, u32[]{:S(2)}) %copy-start.7) | copy-done | bytes 147480
  21.2 0.8 %copy-done.9 = bf16[2,9,6,384]{3,2,1,0:T(8,128)(2,1)S(1)} copy-done((bf16[2,9,6,384]{3,2,1,0:T(8,128)(2,1)S(1)}, bf16[2,9,6,384]{3,2,1,0:T(8,128)(2,1)}, u32[]{:S(2)}) %copy-start.9) | copy-done | bytes 82968
  22.3 0.9 %copy-done.2 = s32[192,768]{1,0:T(8,128)S(1)} copy-done((s32[192,768]{1,0:T(8,128)S(1)}, s32[192,768]{1,0:T(8,128)}, u32[]{:S(2)}) %copy-start.2) | copy-done | bytes 589848
  23.3 0.9 %copy-done.8 = s32[192,192]{1,0:T(8,128)S(1)} copy-done((s32[192,192]{1,0:T(8,128)S(1)}, s32[192,192]{1,0:T(8,128)}, u32[]{:S(2)}) %copy-start.8) | copy-done | bytes 147480
  24.2 6.5 %block.1 = (bf16[288,192]{1,0:T(8,128)(2,1)S(1)}, bf16[288,192]{1,0:T(8,128)(2,1)S(1)}, bf16[3584,128]{1,0:T(8,128)(2,1)S(1)}) custom-call(s32[12]{0:T(128)S(1)} %pad_add_fusion.2.scalars_ref, bf16[288,192]{1,0:T(8,128)(2,1)S(1)} %get-tuple-element.69.start_ref, bf16[288,192]{1,0:T(8,128)(2,1)S(1)} %get-tuple-element.68.d_out_ref, ...), custom_call_target="tpu_custom_call" | custom-call | tf_op jit(solution)/shard_map/block/pallas_call | solution.py:503
  31.1 25.4 %reduce_and_push.1 = (bf16[192,576]{1,0:T(8,128)(2,1)S(1)}, bf16[192,192]{1,0:T(8,128)(2,1)S(1)}, bf16[192,768]{1,0:T(8,128)(2,1)S(1)}, bf16[192,768]{1,0:T(8,128)(2,1)S(1)}, bf16[208,384]{1,0:T(8,128)(2,1)S(1)}) custom-call(bf16[3584,128]{1,0:T(8,128)(2,1)S(1)} %get-tuple-element.28.totals_ref, bf16[208,384]{1,0:T(8,128)(2,1)S(1)} %fusion.10.rim_ref), custom_call_target="tpu_custom_call" | custom-call | tf_op jit(solution)/shard_map/reduce_and_push/pallas_call | solution.py:528
  56.9 0.8 %copy.58 = bf16[2,12,12,192]{3,0,2,1:T(2,128)(2,1)} copy(bf16[2,12,12,192]{3,2,1,0:T(8,128)(2,1)S(1)} %get-tuple-element.58) | data formatting | bytes 221184
  58.4 0.3 multiply_reduce_fusion
  59.7 0.7 %copy.57 = bf16[2,6,6,384]{3,0,2,1:T(2,128)(2,1)} copy(bf16[2,6,6,384]{3,2,1,0:T(8,128)(2,1)S(1)} %reshape.159) | data formatting | bytes 110592
  60.3 0.7 %copy.67 = bf16[192,576]{1,0:T(8,128)(2,1)} copy(bf16[192,576]{1,0:T(8,128)(2,1)S(1)} %get-tuple-element.86) | data formatting | bytes 442368
  61.0 0.6 %copy.68 = bf16[192,192]{1,0:T(8,128)(2,1)} copy(bf16[192,192]{1,0:T(8,128)(2,1)S(1)} %get-tuple-element.87) | data formatting | bytes 147456
  61.7 0.7 %copy.69 = bf16[192,768]{1,0:T(8,128)(2,1)} copy(bf16[192,768]{1,0:T(8,128)(2,1)S(1)} %get-tuple-element.88) | data formatting | bytes 589824
  62.4 0.7 %copy.70 = bf16[768,192]{0,1:T(8,128)(2,1)} copy(bf16[768,192]{0,1:T(8,128)(2,1)S(1)} %bitcast.21) | data formatting | bytes 589824
  (74 shorter events, 3.9 us)
Async XLA Ops:
  0.6 58.7 %copy-start = (bf16[768,384]{1,0:T(8,128)(2,1)S(1)}, bf16[768,384]{1,0:T(8,128)(2,1)}, u32[]{:S(2)}) copy-start(bf16[768,384]{1,0:T(8,128)(2,1)} %param.21) | copy-start | bytes 1769476
  0.8 0.7 %copy-start.13 = (s32[4]{0:T(128)S(1)}, s32[4]{0:T(128)}, u32[]{:S(2)}) copy-start(s32[4]{0:T(128)} %param.18) | copy-start | bytes 52
  0.8 0.7 %copy-start.14 = (s32[4]{0:T(128)S(1)}, s32[4]{0:T(128)}, u32[]{:S(2)}) copy-start(s32[4]{0:T(128)} %param.17) | copy-start | bytes 52
  2.5 0.9 %copy-start.12 = (s32[20736]{0:T(1024)S(1)}, s32[20736]{0:T(1024)}, u32[]{:S(2)}) copy-start(s32[20736]{0:T(1024)} %param.20) | copy-start | bytes 248836
  3.9 0.9 %copy-start.10 = (bf16[2,12,12,192]{3,0,2,1:T(2,128)(2,1)S(1)}, bf16[2,12,12,192]{3,0,2,1:T(2,128)(2,1)}, u32[]{:S(2)}) copy-start(bf16[2,12,12,192]{3,0,2,1:T(2,128)(2,1)} %param.11) | copy-start | bytes 331780
  4.8 0.9 %copy-start.11 = (bf16[2,12,12,192]{3,0,2,1:T(2,128)(2,1)S(1)}, bf16[2,12,12,192]{3,0,2,1:T(2,128)(2,1)}, u32[]{:S(2)}) copy-start(bf16[2,12,12,192]{3,0,2,1:T(2,128)(2,1)} %param.12) | copy-start | bytes 331780
  5.8 1.1 %copy-start.3 = (s32[192,768]{1,0:T(8,128)S(1)}, s32[192,768]{1,0:T(8,128)}, u32[]{:S(2)}) copy-start(s32[192,768]{1,0:T(8,128)} %up_far.1) | copy-start | bytes 1769476
  6.6 1.0 %copy-start.6 = (s32[192,192]{1,0:T(8,128)S(1)}, s32[192,192]{1,0:T(8,128)}, u32[]{:S(2)}) copy-start(s32[192,192]{1,0:T(8,128)} %proj_far.1) | copy-start | bytes 442372
  7.6 1.1 %copy-start.4 = (s32[768,192]{0,1:T(8,128)S(1)}, s32[768,192]{0,1:T(8,128)}, u32[]{:S(2)}) copy-start(s32[768,192]{0,1:T(8,128)} %param.16) | copy-start | bytes 1769476
  8.7 1.0 %copy-start.5 = (s32[192,576]{1,0:T(8,128)S(1)}, s32[192,576]{1,0:T(8,128)}, u32[]{:S(2)}) copy-start(s32[192,576]{1,0:T(8,128)} %qkv_far.1) | copy-start | bytes 1327108
  19.6 0.8 %copy-start.1 = (s32[192,768]{1,0:T(8,128)}, s32[192,768]{1,0:T(8,128)S(1)}, u32[]{:S(2)}) copy-start(s32[192,768]{1,0:T(8,128)S(1)} %get-tuple-element.24.down_ref) | copy-start | bytes 1769476
  20.4 0.7 %copy-start.7 = (s32[192,192]{1,0:T(8,128)}, s32[192,192]{1,0:T(8,128)S(1)}, u32[]{:S(2)}) copy-start(s32[192,192]{1,0:T(8,128)S(1)} %get-tuple-element.22.proj_ref) | copy-start | bytes 442372
  21.1 0.9 %copy-start.9 = (bf16[2,9,6,384]{3,2,1,0:T(8,128)(2,1)S(1)}, bf16[2,9,6,384]{3,2,1,0:T(8,128)(2,1)}, u32[]{:S(2)}) copy-start(bf16[2,9,6,384]{3,2,1,0:T(8,128)(2,1)} %get-tuple-element.65) | copy-start | bytes 248836
  22.2 1.1 %copy-start.2 = (s32[192,768]{1,0:T(8,128)S(1)}, s32[192,768]{1,0:T(8,128)}, u32[]{:S(2)}) copy-start(s32[192,768]{1,0:T(8,128)} %copy-done.1) | copy-start | bytes 1769476
  23.3 0.9 %copy-start.8 = (s32[192,192]{1,0:T(8,128)S(1)}, s32[192,192]{1,0:T(8,128)}, u32[]{:S(2)}) copy-start(s32[192,192]{1,0:T(8,128)} %copy-done.7) | copy-start | bytes 442372

commit v5 on v4

--- a/solution.py
+++ b/solution.py
@@ -64,26 +64,12 @@
     rim_ref,
     index_ref,
     table_ref,
-    qkv_far,
-    proj_far,
-    up_far,
-    down_far,
     rim_out_ref,
     bias_ref,
-    qkv_ref,
-    proj_ref,
-    up_ref,
-    down_ref,
     rim_in,
     sends,
     receives,
-    fetches,
 ):
-    pairs = [(qkv_far, qkv_ref), (proj_far, proj_ref), (up_far, up_ref), (down_far, down_ref)]
-    fetched = []
-    for slot, (source, target) in enumerate(pairs):
-        fetched.append(pltpu.make_async_copy(source, target, fetches.at[slot]))
-        fetched[-1].start()
     behind, ahead = neighbours(lon_count, lat_count)
     greet(behind + ahead)
     copies = []
@@ -123,8 +109,6 @@
         return carry
 
     lax.fori_loop(0, steps, one_step, 0)
-    for copy in fetched:
-        copy.wait()
     for copy in copies:
         copy.wait_recv()
     rim_out_ref[...] = rim_in[...]
@@ -150,10 +134,10 @@
     start_ref,
     d_out_ref,
     qkv_ref,
+    bias_ref,
     proj_ref,
     up_ref,
     down_ref,
-    bias_ref,
     final_ref,
     grad_ref,
     totals_ref,
@@ -169,13 +153,12 @@
         factor = math.sqrt(C / fan_in) / scale
         return (jnp.clip(codes, -largest, largest).astype(F32) * factor).astype(BF16)
 
+    start = start_ref[...].astype(F32)
+    center, inverse = center_of(start)
+    normed = (center * inverse).astype(BF16)
     w_q = dequant(qkv_ref[:, :C], 0, C)
     w_k = dequant(qkv_ref[:, C : 2 * C], 0, C)
     w_v = dequant(qkv_ref[:, 2 * C :], 0, C)
-    w_proj = dequant(proj_ref[...], 1, C)
-    start = start_ref[...].astype(F32)
-    center, inverse = center_of(start)
-    normed = (center * inverse).astype(BF16)
     q = nn(normed, w_q).astype(BF16)
     k = nn(normed, w_k).astype(BF16)
     v = nn(normed, w_v).astype(BF16)
@@ -211,6 +194,7 @@
         heads_s[part, :] = unstack(nn(weights.astype(BF16), v[part]))
 
     heads = heads_s[...].astype(BF16)
+    w_proj = dequant(proj_ref[...], 1, C)
     resid = (start + nn(heads, w_proj)).astype(BF16)
     center_two, inverse_two = center_of(resid.astype(F32))
     normed_two = (center_two * inverse_two).astype(BF16)
@@ -469,27 +453,27 @@
     table = jnp.pad(table, spare).reshape(piece_rows, pieces, PIECE).transpose(1, 0, 2)
     vmem = pl.BlockSpec(memory_space=pltpu.VMEM)
     smem = pl.BlockSpec(memory_space=pltpu.SMEM)
-    codes = (qkv_codes, proj_codes, up_codes, down_codes.T)
-    pulled, bias, *codes = pl.pallas_call(
+    pulled, bias = pl.pallas_call(
         functools.partial(pull_kernel, lon_count, lat_count, lengths),
         out_shape=[
             jax.ShapeDtypeStruct(pulled.shape, BF16),
             jax.ShapeDtypeStruct((table_rows, WTOK, LANES), F32),
-        ]
-        + [jax.ShapeDtypeStruct(code.shape, jnp.int32) for code in codes],
-        in_specs=[vmem] * 3 + [pl.BlockSpec(memory_space=pl.ANY)] * 4,
-        out_specs=[vmem] * 6,
+        ],
+        in_specs=[vmem] * 3,
+        out_specs=[vmem] * 2,
         scratch_shapes=[
             pltpu.VMEM(pulled.shape, BF16),
             pltpu.SemaphoreType.DMA((len(lengths),)),
             pltpu.SemaphoreType.DMA((len(lengths),)),
-            pltpu.SemaphoreType.DMA((len(codes),)),
         ],
         compiler_params=pltpu.CompilerParams(
-            collective_id=1, has_side_effects=True, vmem_limit_bytes=48 * 2**20
+            collective_id=1, has_side_effects=True, vmem_limit_bytes=32 * 2**20
+        ),
+        cost_estimate=pl.CostEstimate(
+            flops=2 * table.size * index.size, bytes_accessed=20 * 10**6, transcendentals=0
         ),
         name="pull_and_bias",
-    )(pulled, index, table, *codes)
+    )(pulled, index, table)
     got = unpack(pulled)
     upper = jnp.concatenate([got[2], got[1]], axis=2)
     lower = jnp.concatenate([got[0], both[:, :-rim_rows, :rim_cols]], axis=2)
@@ -497,6 +481,7 @@
 
     first_row = lat_start + WLAT * jnp.arange(window_rows, dtype=jnp.int32)
     edges = jnp.stack([-first_row * WLON, (lat_limit - first_row) * WLON], axis=1).reshape(-1)
+    operands = (qkv_codes, bias, proj_codes, up_codes, down_codes.T)
     wide = jax.ShapeDtypeStruct((token_count, feat_count), BF16)
     chunk = -(-TOTAL_ROWS // (lon_count * lat_count * 16)) * 16
     total_rows = chunk * lon_count * lat_count
@@ -507,14 +492,16 @@
         out_specs=[vmem] * 3,
         scratch_shapes=[pltpu.VMEM((token_count, feat_count), F32)] * 4
         + [pltpu.VMEM((C, 4 * C), F32)],
-        compiler_params=pltpu.CompilerParams(vmem_limit_bytes=48 * 2**20),
+        compiler_params=pltpu.CompilerParams(vmem_limit_bytes=32 * 2**20),
+        cost_estimate=pl.CostEstimate(
+            flops=2 * 10**9, bytes_accessed=20 * 10**6, transcendentals=10**6
+        ),
         name="block",
     )(
         jnp.concatenate([bit_widths, quant_scales, edges]),
         frame[:, :feat_count],
         frame[:, feat_count:],
-        *codes,
-        bias,
+        *operands,
     )
     frame = jnp.concatenate([final, grad], axis=-1).reshape(grid_shape + (-1,))
     rim, lengths, unpack = packed(
@@ -551,6 +538,9 @@
         compiler_params=pltpu.CompilerParams(
             collective_id=0, has_side_effects=True, vmem_limit_bytes=48 * 2**20
         ),
+        cost_estimate=pl.CostEstimate(
+            flops=10**7, bytes_accessed=60 * 10**6, transcendentals=0
+        ),
         name="reduce_and_push",
     )(totals, rim)
     got = unpack(rim)

time: 63.6 us -> 58 us (0.912)
  local copies, waits for them, and re-layouts: 18.6 us -> 14 us
  Pallas kernels: 41.8 us -> 41 us
    unnamed x39 -> x33, local copies, waits for them, and re-layouts: 15.7 us -> 11.7 us
    pallas_call x1, Pallas kernels: 9.87 us -> 9.06 us  [per_device(): pl.pallas_call(functools.partial(pull_kernel, lon_count, lat_count, lengt...]
where the time goes in v5:
time: 58 us; the launch traced here: 57.7 us
  Pallas kernels  41 us (71%)
  local copies, waits for them, and re-layouts  14 us (24%)
  other arithmetic  1.34 us (2%)
  between operations  1.08 us (2%)
    pallas_call x1, Pallas kernels, per_device(): pl.pallas_call(functools.partial(reduce_kernel, lon_count, lat_count, len...  25.4 us
    unnamed x33, local copies, waits for them, and re-layouts  11.7 us
    pallas_call x1, Pallas kernels, per_device(): pl.pallas_call(functools.partial(pull_kernel, lon_count, lat_count, lengt...  9.06 us
    pallas_call x1, Pallas kernels, per_device(): pl.pallas_call(functools.partial(block_kernel, window_rows), out_shape=[w...  6.54 us

profile of v5, /device:TPU:1, one launch (start us, length us, event | category | flops | bytes accessed | tf_op | source)
XLA Modules:
  0.0 57.7 jit_solution(3033527792714060551)
XLA Ops:
  0.8 0.6 %copy-done.10 = s32[4]{0:T(128)S(1)} copy-done((s32[4]{0:T(128)S(1)}, s32[4]{0:T(128)}, u32[]{:S(2)}) %copy-start.10) | copy-done | bytes 40
  1.6 0.9 %copy.51 = bf16[2,1,6,3312]{3,2,0,1:T(8,128)(2,1)S(1)} copy(bf16[2,1,6,3312]{3,0,2,1:T(2,128)(2,1)} %param.19) | data formatting | bytes 158976 | tf_op args[8]
  2.6 0.9 %copy-done.9 = s32[20736]{0:T(1024)S(1)} copy-done((s32[20736]{0:T(1024)S(1)}, s32[20736]{0:T(1024)}, u32[]{:S(2)}) %copy-start.9) | copy-done | bytes 82968
  3.4 0.3 reshape.144
  3.9 0.9 %copy-done.7 = bf16[2,12,12,192]{3,0,2,1:T(2,128)(2,1)S(1)} copy-done((bf16[2,12,12,192]{3,0,2,1:T(2,128)(2,1)S(1)}, bf16[2,12,12,192]{3,0,2,1:T(2,128)(2,1)}, u32[]{:S(2)}) %copy-start.7) | copy-done | bytes 110616
  4.8 0.9 %copy-done.8 = bf16[2,12,12,192]{3,0,2,1:T(2,128)(2,1)S(1)} copy-done((bf16[2,12,12,192]{3,0,2,1:T(2,128)(2,1)S(1)}, bf16[2,12,12,192]{3,0,2,1:T(2,128)(2,1)}, u32[]{:S(2)}) %copy-start.8) | copy-done | bytes 110616
  6.0 9.1 %pull_and_bias.1 = (bf16[208,384]{1,0:T(8,128)(2,1)S(1)}, f32[12,144,128]{2,1,0:T(8,128)S(1)}) custom-call(bf16[208,384]{1,0:T(8,128)(2,1)S(1)} %fusion.8.rim_ref, s32[12,1536]{1,0:T(8,128)S(1)} %reshape.145.index_ref, bf16[13,16,256]{2,1,0:T(8,128)(2,1)S(1)} %bitcast.20), custom_call_target="tpu_custom_call" | custom-call | flops 1962934272 | bytes 20000000 | tf_op jit(solution)/shard_map/pull_and_bias/pallas_call | solution.py:456
  15.1 0.9 %copy-done.5 = f32[12,144,128]{2,1,0:T(8,128)} copy-done((f32[12,144,128]{2,1,0:T(8,128)}, f32[12,144,128]{2,1,0:T(8,128)S(1)}, u32[]{:S(2)}) %copy-start.5) | copy-done | bytes 884760
  16.4 0.5 copy-done.4
  17.0 0.3 copy-done.2
  17.2 0.2 copy-done.1
  17.6 1.2 %copy-done.6 = f32[12,144,128]{2,1,0:T(8,128)S(1)} copy-done((f32[12,144,128]{2,1,0:T(8,128)S(1)}, f32[12,144,128]{2,1,0:T(8,128)}, u32[]{:S(2)}) %copy-start.6) | copy-done | bytes 884760
  18.7 6.5 %block.1 = (bf16[288,192]{1,0:T(8,128)(2,1)S(1)}, bf16[288,192]{1,0:T(8,128)(2,1)S(1)}, bf16[3584,128]{1,0:T(8,128)(2,1)S(1)}) custom-call(s32[12]{0:T(128)S(1)} %pad_add_fusion.2.scalars_ref, bf16[288,192]{1,0:T(8,128)(2,1)S(1)} %get-tuple-element.61.start_ref, bf16[288,192]{1,0:T(8,128)(2,1)S(1)} %get-tuple-element.60.d_out_ref, s32[192,576]{1,0:T(8,128)S(1)} %copy-done.3, ...), custom_call_target="tpu_custom_call" | custom-call | flops 2000000000 | bytes 20000000 | tf_op jit(solution)/shard_map/block/pallas_call | solution.py:488
  25.6 25.4 %reduce_and_push.1 = (bf16[192,576]{1,0:T(8,128)(2,1)S(1)}, bf16[192,192]{1,0:T(8,128)(2,1)S(1)}, bf16[192,768]{1,0:T(8,128)(2,1)S(1)}, bf16[192,768]{1,0:T(8,128)(2,1)S(1)}, bf16[208,384]{1,0:T(8,128)(2,1)S(1)}) custom-call(bf16[3584,128]{1,0:T(8,128)(2,1)S(1)} %get-tuple-element.20.totals_ref, bf16[208,384]{1,0:T(8,128)(2,1)S(1)} %fusion.10.rim_ref), custom_call_target="tpu_custom_call" | custom-call | flops 10000000 | bytes 60000000 | tf_op jit(solution)/shard_map/reduce_and_push/pallas_call | solution.py:515
  51.5 0.8 %copy.58 = bf16[2,12,12,192]{3,0,2,1:T(2,128)(2,1)} copy(bf16[2,12,12,192]{3,2,1,0:T(8,128)(2,1)S(1)} %get-tuple-element.50) | data formatting | bytes 221184
  52.3 0.2 copy.53
  52.9 0.3 multiply_reduce_fusion
  53.4 0.3 reshape.160
  53.9 0.3 convolution_convert_fusion
  54.2 0.7 %copy.57 = bf16[2,6,6,384]{3,0,2,1:T(2,128)(2,1)} copy(bf16[2,6,6,384]{3,2,1,0:T(8,128)(2,1)S(1)} %reshape.159) | data formatting | bytes 110592
  54.9 0.7 %copy.67 = bf16[192,576]{1,0:T(8,128)(2,1)} copy(bf16[192,576]{1,0:T(8,128)(2,1)S(1)} %get-tuple-element.78) | data formatting | bytes 442368
  55.6 0.6 %copy.68 = bf16[192,192]{1,0:T(8,128)(2,1)} copy(bf16[192,192]{1,0:T(8,128)(2,1)S(1)} %get-tuple-element.79) | data formatting | bytes 147456
  56.2 0.7 %copy.69 = bf16[192,768]{1,0:T(8,128)(2,1)} copy(bf16[192,768]{1,0:T(8,128)(2,1)S(1)} %get-tuple-element.80) | data formatting | bytes 589824
  57.0 0.7 %copy.70 = bf16[768,192]{0,1:T(8,128)(2,1)} copy(bf16[768,192]{0,1:T(8,128)(2,1)S(1)} %bitcast.19) | data formatting | bytes 589824
  (68 shorter events, 2.7 us)
Async XLA Ops:
  0.6 53.3 %copy-start = (bf16[768,384]{1,0:T(8,128)(2,1)S(1)}, bf16[768,384]{1,0:T(8,128)(2,1)}, u32[]{:S(2)}) copy-start(bf16[768,384]{1,0:T(8,128)(2,1)} %param.21) | copy-start | bytes 1769476
  0.8 0.7 %copy-start.10 = (s32[4]{0:T(128)S(1)}, s32[4]{0:T(128)}, u32[]{:S(2)}) copy-start(s32[4]{0:T(128)} %param.18) | copy-start | bytes 52
  0.8 0.7 %copy-start.11 = (s32[4]{0:T(128)S(1)}, s32[4]{0:T(128)}, u32[]{:S(2)}) copy-start(s32[4]{0:T(128)} %param.17) | copy-start | bytes 52
  2.5 0.9 %copy-start.9 = (s32[20736]{0:T(1024)S(1)}, s32[20736]{0:T(1024)}, u32[]{:S(2)}) copy-start(s32[20736]{0:T(1024)} %param.20) | copy-start | bytes 248836
  3.9 0.9 %copy-start.7 = (bf16[2,12,12,192]{3,0,2,1:T(2,128)(2,1)S(1)}, bf16[2,12,12,192]{3,0,2,1:T(2,128)(2,1)}, u32[]{:S(2)}) copy-start(bf16[2,12,12,192]{3,0,2,1:T(2,128)(2,1)} %param.11) | copy-start | bytes 331780
  4.8 0.9 %copy-start.8 = (bf16[2,12,12,192]{3,0,2,1:T(2,128)(2,1)S(1)}, bf16[2,12,12,192]{3,0,2,1:T(2,128)(2,1)}, u32[]{:S(2)}) copy-start(bf16[2,12,12,192]{3,0,2,1:T(2,128)(2,1)} %param.12) | copy-start | bytes 331780
  15.1 0.9 %copy-start.5 = (f32[12,144,128]{2,1,0:T(8,128)}, f32[12,144,128]{2,1,0:T(8,128)S(1)}, u32[]{:S(2)}) copy-start(f32[12,144,128]{2,1,0:T(8,128)S(1)} %get-tuple-element.17.bias_ref) | copy-start | bytes 2654212
  16.0 0.9 %copy-start.4 = (s32[192,192]{1,0:T(8,128)S(1)}, s32[192,192]{1,0:T(8,128)}, u32[]{:S(2)}) copy-start(s32[192,192]{1,0:T(8,128)} %proj_ref.1) | copy-start | bytes 442372
  16.1 1.1 %copy-start.2 = (s32[768,192]{0,1:T(8,128)S(1)}, s32[768,192]{0,1:T(8,128)}, u32[]{:S(2)}) copy-start(s32[768,192]{0,1:T(8,128)} %param.16) | copy-start | bytes 1769476
  16.2 1.2 %copy-start.1 = (s32[192,768]{1,0:T(8,128)S(1)}, s32[192,768]{1,0:T(8,128)}, u32[]{:S(2)}) copy-start(s32[192,768]{1,0:T(8,128)} %up_ref.1) | copy-start | bytes 1769476
  16.3 1.3 %copy-start.3 = (s32[192,576]{1,0:T(8,128)S(1)}, s32[192,576]{1,0:T(8,128)}, u32[]{:S(2)}) copy-start(s32[192,576]{1,0:T(8,128)} %qkv_ref.1) | copy-start | bytes 1327108
  17.6 1.2 %copy-start.6 = (f32[12,144,128]{2,1,0:T(8,128)S(1)}, f32[12,144,128]{2,1,0:T(8,128)}, u32[]{:S(2)}) copy-start(f32[12,144,128]{2,1,0:T(8,128)} %copy-done.5) | copy-start | bytes 2654212

commit v6 on v5

--- a/solution.py
+++ b/solution.py
@@ -19,7 +19,8 @@
 HALF = 72
 LANES = 128
 PIECE = 256
-STEPS = 12
+STEPS = 7
+TAIL = 16
 EPSILON = 1e-05
 MASKED = -1000000000.0
 UP_AT = 6 * C
@@ -93,8 +94,9 @@
     tables = table_ref[...].reshape(pieces * piece_rows, piece)
     inside = lax.broadcasted_iota(jnp.int32, (piece, width), 0)
 
-    def one_step(step, carry):
-        index = index_ref[pl.ds(step, 1), :]
+    tiles = width // LANES
+
+    def values_of(index):
         low = jnp.bitwise_and(index, piece - 1)
         high = jnp.right_shift(index, piece.bit_length() - 1)
         chosen = jnp.where(inside == low, 1.0, 0.0).astype(BF16)
@@ -102,13 +104,25 @@
         total = found[:piece_rows]
         for p in range(1, pieces):
             total = jnp.where(high == p, found[p * piece_rows : (p + 1) * piece_rows], total)
-        for i in range(width // LANES):
+        return total
+
+    def one_step(step, carry):
+        total = values_of(index_ref[pl.ds(step, 1), :])
+        for i in range(tiles):
             for r in range(table_rows):
                 row = total[r : r + 1, i * LANES : (i + 1) * LANES]
-                bias_ref[r, pl.ds(step * (width // LANES) + i, 1), :] = row
+                bias_ref[r, pl.ds(step * tiles + i, 1), :] = row
         return carry
 
-    lax.fori_loop(0, steps, one_step, 0)
+    lax.fori_loop(0, steps - 1, one_step, 0)
+    total = values_of(index_ref[steps - 1 : steps, :])
+    group = LANES // TAIL
+    for q in range(HALF):
+        tile = total[:, q // group * LANES : (q // group + 1) * LANES]
+        if q % group:
+            tile = pltpu.roll(tile, LANES - q % group * TAIL, 1)
+        for r in range(table_rows):
+            bias_ref[r, HALF + q : HALF + q + 1, :] = tile[r : r + 1]
     for copy in copies:
         copy.wait_recv()
     rim_out_ref[...] = rim_in[...]
@@ -183,8 +197,13 @@
         level, a = b // window_rows, b % window_rows
         part = slice(b * HALF, (b + 1) * HALF)
         stacked_q = stack(q[part])
-        bias = bias_ref[a * HEADS : (a + 1) * HEADS, (1 - level) * HALF : (2 - level) * HALF, :]
-        bias = bias.reshape(HEADS * HALF, LANES)[:, :HALF]
+        table = bias_ref[a * HEADS : (a + 1) * HEADS, :, :]
+        wide = table[:, :HALF, :].reshape(HEADS * HALF, LANES)
+        tail = table[:, HALF:, :].reshape(HEADS * HALF, LANES)
+        wide_at, tail_at = (1 - level) * (LANES // 2), (1 - level) * (TAIL // 2)
+        bias = jnp.concatenate(
+            [wide[:, wide_at : wide_at + LANES // 2], tail[:, tail_at : tail_at + TAIL // 2]], axis=1
+        )
         scores = nt(stacked_q, k[part]) * HEAD_DIM ** (-0.5) + bias
         allowed = (keys >= scalars_ref[8 + 2 * a]) & (keys < scalars_ref[9 + 2 * a])
         scores = jnp.where(allowed, scores, MASKED)
@@ -443,8 +462,14 @@
         [both[:, :-rim_rows, rim_cols:], both[:, -rim_rows:, :rim_cols], both[:, -rim_rows:, rim_cols:]]
     )
     pair = bias_index.reshape(2, HALF, 2, HALF)
-    index = jnp.concatenate([pair[0, :, 0], pair[1, :, 1]], axis=0)
-    index = jnp.pad(index, ((0, 0), (0, LANES - HALF))).reshape(STEPS, -1)
+    upper, lower = pair[0, :, 0], pair[1, :, 1]
+    cut = LANES // 2
+    wide = jnp.concatenate([upper[:, :cut], lower[:, :cut]], axis=1)
+    tail = jnp.concatenate([upper[:, cut:], lower[:, cut:]], axis=1).reshape(-1, LANES)
+    index = jnp.concatenate([wide, tail], axis=0)
+    tiles = HALF // (STEPS - 1)
+    index = jnp.pad(index, ((0, STEPS * tiles - index.shape[0]), (0, 0)))
+    index = index.reshape(STEPS, tiles * LANES)
     positions = bias_table.shape[-1]
     table_rows = window_rows * HEADS
     pieces, piece_rows = -(-positions // PIECE), -(-table_rows // 16) * 16

time: 58 us -> 60.5 us (1.043)
  Pallas kernels: 41 us -> 43.2 us
    pallas_call x1, Pallas kernels: 6.54 us -> 8.72 us  [per_device(): pl.pallas_call(functools.partial(block_kernel, window_rows), out_shape=[w...]
where the time goes in v6:
time: 60.5 us; the launch traced here: 60.1 us
  Pallas kernels  43.2 us (71%)
  local copies, waits for them, and re-layouts  14.1 us (23%)
  other arithmetic  1.5 us (2%)
  between operations  1.07 us (2%)
    pallas_call x1, Pallas kernels, per_device(): pl.pallas_call(functools.partial(reduce_kernel, lon_count, lat_count, len...  25.4 us
    unnamed x33, local copies, waits for them, and re-layouts  11.6 us
    pallas_call x1, Pallas kernels, per_device(): pl.pallas_call(functools.partial(pull_kernel, lon_count, lat_count, lengt...  9.06 us
    pallas_call x1, Pallas kernels, per_device(): pl.pallas_call(functools.partial(block_kernel, window_rows), out_shape=[w...  8.72 us

profile of v6, /device:TPU:1, one launch (start us, length us, event | category | flops | bytes accessed | tf_op | source)
XLA Modules:
  0.0 60.1 jit_solution(12827422966155942922)
XLA Ops:
  0.8 0.6 %copy-done.10 = s32[4]{0:T(128)S(1)} copy-done((s32[4]{0:T(128)S(1)}, s32[4]{0:T(128)}, u32[]{:S(2)}) %copy-start.10) | copy-done | bytes 40
  1.6 0.9 %copy.65 = bf16[2,1,6,3312]{3,2,0,1:T(8,128)(2,1)S(1)} copy(bf16[2,1,6,3312]{3,0,2,1:T(2,128)(2,1)} %param.19) | data formatting | bytes 158976 | tf_op args[8]
  2.6 0.9 %copy-done.9 = s32[20736]{0:T(1024)S(1)} copy-done((s32[20736]{0:T(1024)S(1)}, s32[20736]{0:T(1024)}, u32[]{:S(2)}) %copy-start.9) | copy-done | bytes 82968
  3.4 0.3 reshape.147
  4.3 0.8 %copy-done.7 = bf16[2,12,12,192]{3,0,2,1:T(2,128)(2,1)S(1)} copy-done((bf16[2,12,12,192]{3,0,2,1:T(2,128)(2,1)S(1)}, bf16[2,12,12,192]{3,0,2,1:T(2,128)(2,1)}, u32[]{:S(2)}) %copy-start.7) | copy-done | bytes 110616
  5.1 0.9 %copy-done.8 = bf16[2,12,12,192]{3,0,2,1:T(2,128)(2,1)S(1)} copy-done((bf16[2,12,12,192]{3,0,2,1:T(2,128)(2,1)S(1)}, bf16[2,12,12,192]{3,0,2,1:T(2,128)(2,1)}, u32[]{:S(2)}) %copy-start.8) | copy-done | bytes 110616
  6.3 9.1 %pull_and_bias.1 = (bf16[208,384]{1,0:T(8,128)(2,1)S(1)}, f32[12,144,128]{2,1,0:T(8,128)S(1)}) custom-call(bf16[208,384]{1,0:T(8,128)(2,1)S(1)} %fusion.8.rim_ref, s32[7,1536]{1,0:T(8,128)S(1)} %reshape.149.index_ref, bf16[13,16,256]{2,1,0:T(8,128)(2,1)S(1)} %bitcast.22), custom_call_target="tpu_custom_call" | custom-call | flops 1145044992 | bytes 20000000 | tf_op jit(solution)/shard_map/pull_and_bias/pallas_call | solution.py:481
  15.4 0.9 %copy-done.5 = f32[12,144,128]{2,1,0:T(8,128)} copy-done((f32[12,144,128]{2,1,0:T(8,128)}, f32[12,144,128]{2,1,0:T(8,128)S(1)}, u32[]{:S(2)}) %copy-start.5) | copy-done | bytes 884760
  16.8 0.5 copy-done.4
  17.3 0.3 copy-done.2
  17.5 0.2 copy-done.1
  17.9 1.2 %copy-done.6 = f32[12,144,128]{2,1,0:T(8,128)S(1)} copy-done((f32[12,144,128]{2,1,0:T(8,128)S(1)}, f32[12,144,128]{2,1,0:T(8,128)}, u32[]{:S(2)}) %copy-start.6) | copy-done | bytes 884760
  19.1 8.7 %block.1 = (bf16[288,192]{1,0:T(8,128)(2,1)S(1)}, bf16[288,192]{1,0:T(8,128)(2,1)S(1)}, bf16[3584,128]{1,0:T(8,128)(2,1)S(1)}) custom-call(s32[12]{0:T(128)S(1)} %pad_add_fusion.3.scalars_ref, bf16[288,192]{1,0:T(8,128)(2,1)S(1)} %get-tuple-element.67.start_ref, bf16[288,192]{1,0:T(8,128)(2,1)S(1)} %get-tuple-element.66.d_out_ref, s32[192,576]{1,0:T(8,128)S(1)} %copy-done.3, ...), custom_call_target="tpu_custom_call" | custom-call | flops 2000000000 | bytes 20000000 | tf_op jit(solution)/shard_map/block/pallas_call | solution.py:513
  28.1 25.4 %reduce_and_push.1 = (bf16[192,576]{1,0:T(8,128)(2,1)S(1)}, bf16[192,192]{1,0:T(8,128)(2,1)S(1)}, bf16[192,768]{1,0:T(8,128)(2,1)S(1)}, bf16[192,768]{1,0:T(8,128)(2,1)S(1)}, bf16[208,384]{1,0:T(8,128)(2,1)S(1)}) custom-call(bf16[3584,128]{1,0:T(8,128)(2,1)S(1)} %get-tuple-element.20.totals_ref, bf16[208,384]{1,0:T(8,128)(2,1)S(1)} %fusion.10.rim_ref), custom_call_target="tpu_custom_call" | custom-call | flops 10000000 | bytes 60000000 | tf_op jit(solution)/shard_map/reduce_and_push/pallas_call | solution.py:540
  53.9 0.8 %copy.72 = bf16[2,12,12,192]{3,0,2,1:T(2,128)(2,1)} copy(bf16[2,12,12,192]{3,2,1,0:T(8,128)(2,1)S(1)} %get-tuple-element.56) | data formatting | bytes 221184
  54.8 0.2 copy.67
  55.4 0.3 multiply_reduce_fusion
  55.9 0.3 reshape.164
  56.4 0.3 convolution_convert_fusion
  56.7 0.7 %copy.71 = bf16[2,6,6,384]{3,0,2,1:T(2,128)(2,1)} copy(bf16[2,6,6,384]{3,2,1,0:T(8,128)(2,1)S(1)} %reshape.163) | data formatting | bytes 110592
  57.4 0.7 %copy.81 = bf16[192,576]{1,0:T(8,128)(2,1)} copy(bf16[192,576]{1,0:T(8,128)(2,1)S(1)} %get-tuple-element.84) | data formatting | bytes 442368
  58.1 0.6 %copy.82 = bf16[192,192]{1,0:T(8,128)(2,1)} copy(bf16[192,192]{1,0:T(8,128)(2,1)S(1)} %get-tuple-element.85) | data formatting | bytes 147456
  58.7 0.7 %copy.83 = bf16[192,768]{1,0:T(8,128)(2,1)} copy(bf16[192,768]{1,0:T(8,128)(2,1)S(1)} %get-tuple-element.86) | data formatting | bytes 589824
  59.4 0.7 %copy.84 = bf16[768,192]{0,1:T(8,128)(2,1)} copy(bf16[768,192]{0,1:T(8,128)(2,1)S(1)} %bitcast.21) | data formatting | bytes 589824
  (72 shorter events, 3.1 us)
Async XLA Ops:
  0.6 55.8 %copy-start = (bf16[768,384]{1,0:T(8,128)(2,1)S(1)}, bf16[768,384]{1,0:T(8,128)(2,1)}, u32[]{:S(2)}) copy-start(bf16[768,384]{1,0:T(8,128)(2,1)} %param.21) | copy-start | bytes 1769476
  0.8 0.7 %copy-start.10 = (s32[4]{0:T(128)S(1)}, s32[4]{0:T(128)}, u32[]{:S(2)}) copy-start(s32[4]{0:T(128)} %param.18) | copy-start | bytes 52
  0.8 0.7 %copy-start.11 = (s32[4]{0:T(128)S(1)}, s32[4]{0:T(128)}, u32[]{:S(2)}) copy-start(s32[4]{0:T(128)} %param.17) | copy-start | bytes 52
  2.5 0.9 %copy-start.9 = (s32[20736]{0:T(1024)S(1)}, s32[20736]{0:T(1024)}, u32[]{:S(2)}) copy-start(s32[20736]{0:T(1024)} %param.20) | copy-start | bytes 248836
  4.2 0.9 %copy-start.7 = (bf16[2,12,12,192]{3,0,2,1:T(2,128)(2,1)S(1)}, bf16[2,12,12,192]{3,0,2,1:T(2,128)(2,1)}, u32[]{:S(2)}) copy-start(bf16[2,12,12,192]{3,0,2,1:T(2,128)(2,1)} %param.11) | copy-start | bytes 331780
  5.1 0.9 %copy-start.8 = (bf16[2,12,12,192]{3,0,2,1:T(2,128)(2,1)S(1)}, bf16[2,12,12,192]{3,0,2,1:T(2,128)(2,1)}, u32[]{:S(2)}) copy-start(bf16[2,12,12,192]{3,0,2,1:T(2,128)(2,1)} %param.12) | copy-start | bytes 331780
  15.4 0.9 %copy-start.5 = (f32[12,144,128]{2,1,0:T(8,128)}, f32[12,144,128]{2,1,0:T(8,128)S(1)}, u32[]{:S(2)}) copy-start(f32[12,144,128]{2,1,0:T(8,128)S(1)} %get-tuple-element.17.bias_ref) | copy-start | bytes 2654212
  16.4 0.9 %copy-start.4 = (s32[192,192]{1,0:T(8,128)S(1)}, s32[192,192]{1,0:T(8,128)}, u32[]{:S(2)}) copy-start(s32[192,192]{1,0:T(8,128)} %proj_ref.1) | copy-start | bytes 442372
  16.4 1.1 %copy-start.2 = (s32[768,192]{0,1:T(8,128)S(1)}, s32[768,192]{0,1:T(8,128)}, u32[]{:S(2)}) copy-start(s32[768,192]{0,1:T(8,128)} %param.16) | copy-start | bytes 1769476
  16.6 1.2 %copy-start.1 = (s32[192,768]{1,0:T(8,128)S(1)}, s32[192,768]{1,0:T(8,128)}, u32[]{:S(2)}) copy-start(s32[192,768]{1,0:T(8,128)} %up_ref.1) | copy-start | bytes 1769476
  16.6 1.3 %copy-start.3 = (s32[192,576]{1,0:T(8,128)S(1)}, s32[192,576]{1,0:T(8,128)}, u32[]{:S(2)}) copy-start(s32[192,576]{1,0:T(8,128)} %qkv_ref.1) | copy-start | bytes 1327108
  17.9 1.2 %copy-start.6 = (f32[12,144,128]{2,1,0:T(8,128)S(1)}, f32[12,144,128]{2,1,0:T(8,128)}, u32[]{:S(2)}) copy-start(f32[12,144,128]{2,1,0:T(8,128)} %copy-done.5) | copy-start | bytes 2654212

commit v7 on v5

--- a/solution.py
+++ b/solution.py
@@ -508,7 +508,7 @@
         [frame[:, rim_rows:, :rim_cols], frame[:, :rim_rows, rim_cols:], frame[:, :rim_rows, :rim_cols]]
     )
     units = chunk // 16
-    chunks = [16 * n for n in (units - units // 2, units // 2) if n]
+    chunks = [16 * n for n in ((units + 2) // 3, (units + 1) // 3, units // 3) if n]
     copies = 2 * (1 + lat_count - 1 + lon_count // 2 - 1) * len(chunks) + len(lengths)
     half = total_rows // 2
     part = half // lat_count

time: 58 us -> 57.4 us (0.990)
  no operation moved by 1% of the time
where the time goes in v7:
time: 57.4 us; the launch traced here: 57.1 us
  Pallas kernels  40.5 us (71%)
  local copies, waits for them, and re-layouts  14 us (24%)
  other arithmetic  1.34 us (2%)
  between operations  1.08 us (2%)
    pallas_call x1, Pallas kernels, per_device(): pl.pallas_call(functools.partial(reduce_kernel, lon_count, lat_count, len...  24.9 us
    unnamed x33, local copies, waits for them, and re-layouts  11.7 us
    pallas_call x1, Pallas kernels, per_device(): pl.pallas_call(functools.partial(pull_kernel, lon_count, lat_count, lengt...  9.06 us
    pallas_call x1, Pallas kernels, per_device(): pl.pallas_call(functools.partial(block_kernel, window_rows), out_shape=[w...  6.54 us

profile of v7, /device:TPU:1, one launch (start us, length us, event | category | flops | bytes accessed | tf_op | source)
XLA Modules:
  0.0 57.1 jit_solution(286172084106381270)
XLA Ops:
  0.8 0.6 %copy-done.10 = s32[4]{0:T(128)S(1)} copy-done((s32[4]{0:T(128)S(1)}, s32[4]{0:T(128)}, u32[]{:S(2)}) %copy-start.10) | copy-done | bytes 40
  1.6 0.9 %copy.51 = bf16[2,1,6,3312]{3,2,0,1:T(8,128)(2,1)S(1)} copy(bf16[2,1,6,3312]{3,0,2,1:T(2,128)(2,1)} %param.19) | data formatting | bytes 158976 | tf_op args[8]
  2.6 0.9 %copy-done.9 = s32[20736]{0:T(1024)S(1)} copy-done((s32[20736]{0:T(1024)S(1)}, s32[20736]{0:T(1024)}, u32[]{:S(2)}) %copy-start.9) | copy-done | bytes 82968
  3.4 0.3 reshape.144
  3.9 0.9 %copy-done.7 = bf16[2,12,12,192]{3,0,2,1:T(2,128)(2,1)S(1)} copy-done((bf16[2,12,12,192]{3,0,2,1:T(2,128)(2,1)S(1)}, bf16[2,12,12,192]{3,0,2,1:T(2,128)(2,1)}, u32[]{:S(2)}) %copy-start.7) | copy-done | bytes 110616
  4.8 0.9 %copy-done.8 = bf16[2,12,12,192]{3,0,2,1:T(2,128)(2,1)S(1)} copy-done((bf16[2,12,12,192]{3,0,2,1:T(2,128)(2,1)S(1)}, bf16[2,12,12,192]{3,0,2,1:T(2,128)(2,1)}, u32[]{:S(2)}) %copy-start.8) | copy-done | bytes 110616
  6.0 9.1 %pull_and_bias.1 = (bf16[208,384]{1,0:T(8,128)(2,1)S(1)}, f32[12,144,128]{2,1,0:T(8,128)S(1)}) custom-call(bf16[208,384]{1,0:T(8,128)(2,1)S(1)} %fusion.8.rim_ref, s32[12,1536]{1,0:T(8,128)S(1)} %reshape.145.index_ref, bf16[13,16,256]{2,1,0:T(8,128)(2,1)S(1)} %bitcast.20), custom_call_target="tpu_custom_call" | custom-call | flops 1962934272 | bytes 20000000 | tf_op jit(solution)/shard_map/pull_and_bias/pallas_call | solution.py:456
  15.1 0.9 %copy-done.5 = f32[12,144,128]{2,1,0:T(8,128)} copy-done((f32[12,144,128]{2,1,0:T(8,128)}, f32[12,144,128]{2,1,0:T(8,128)S(1)}, u32[]{:S(2)}) %copy-start.5) | copy-done | bytes 884760
  16.4 0.5 copy-done.4
  17.0 0.3 copy-done.2
  17.2 0.2 copy-done.1
  17.6 1.2 %copy-done.6 = f32[12,144,128]{2,1,0:T(8,128)S(1)} copy-done((f32[12,144,128]{2,1,0:T(8,128)S(1)}, f32[12,144,128]{2,1,0:T(8,128)}, u32[]{:S(2)}) %copy-start.6) | copy-done | bytes 884760
  18.7 6.5 %block.1 = (bf16[288,192]{1,0:T(8,128)(2,1)S(1)}, bf16[288,192]{1,0:T(8,128)(2,1)S(1)}, bf16[3584,128]{1,0:T(8,128)(2,1)S(1)}) custom-call(s32[12]{0:T(128)S(1)} %pad_add_fusion.2.scalars_ref, bf16[288,192]{1,0:T(8,128)(2,1)S(1)} %get-tuple-element.61.start_ref, bf16[288,192]{1,0:T(8,128)(2,1)S(1)} %get-tuple-element.60.d_out_ref, s32[192,576]{1,0:T(8,128)S(1)} %copy-done.3, ...), custom_call_target="tpu_custom_call" | custom-call | flops 2000000000 | bytes 20000000 | tf_op jit(solution)/shard_map/block/pallas_call | solution.py:488
  25.6 24.9 %reduce_and_push.1 = (bf16[192,576]{1,0:T(8,128)(2,1)S(1)}, bf16[192,192]{1,0:T(8,128)(2,1)S(1)}, bf16[192,768]{1,0:T(8,128)(2,1)S(1)}, bf16[192,768]{1,0:T(8,128)(2,1)S(1)}, bf16[208,384]{1,0:T(8,128)(2,1)S(1)}) custom-call(bf16[3584,128]{1,0:T(8,128)(2,1)S(1)} %get-tuple-element.20.totals_ref, bf16[208,384]{1,0:T(8,128)(2,1)S(1)} %fusion.10.rim_ref), custom_call_target="tpu_custom_call" | custom-call | flops 10000000 | bytes 60000000 | tf_op jit(solution)/shard_map/reduce_and_push/pallas_call | solution.py:515
  50.9 0.8 %copy.58 = bf16[2,12,12,192]{3,0,2,1:T(2,128)(2,1)} copy(bf16[2,12,12,192]{3,2,1,0:T(8,128)(2,1)S(1)} %get-tuple-element.50) | data formatting | bytes 221184
  51.7 0.2 copy.53
  52.4 0.3 multiply_reduce_fusion
  52.9 0.3 reshape.160
  53.4 0.3 convolution_convert_fusion
  53.7 0.7 %copy.57 = bf16[2,6,6,384]{3,0,2,1:T(2,128)(2,1)} copy(bf16[2,6,6,384]{3,2,1,0:T(8,128)(2,1)S(1)} %reshape.159) | data formatting | bytes 110592
  54.4 0.7 %copy.67 = bf16[192,576]{1,0:T(8,128)(2,1)} copy(bf16[192,576]{1,0:T(8,128)(2,1)S(1)} %get-tuple-element.78) | data formatting | bytes 442368
  55.1 0.6 %copy.68 = bf16[192,192]{1,0:T(8,128)(2,1)} copy(bf16[192,192]{1,0:T(8,128)(2,1)S(1)} %get-tuple-element.79) | data formatting | bytes 147456
  55.7 0.7 %copy.69 = bf16[192,768]{1,0:T(8,128)(2,1)} copy(bf16[192,768]{1,0:T(8,128)(2,1)S(1)} %get-tuple-element.80) | data formatting | bytes 589824
  56.4 0.7 %copy.70 = bf16[768,192]{0,1:T(8,128)(2,1)} copy(bf16[768,192]{0,1:T(8,128)(2,1)S(1)} %bitcast.19) | data formatting | bytes 589824
  (68 shorter events, 2.7 us)
Async XLA Ops:
  0.6 52.7 %copy-start = (bf16[768,384]{1,0:T(8,128)(2,1)S(1)}, bf16[768,384]{1,0:T(8,128)(2,1)}, u32[]{:S(2)}) copy-start(bf16[768,384]{1,0:T(8,128)(2,1)} %param.21) | copy-start | bytes 1769476
  0.8 0.7 %copy-start.10 = (s32[4]{0:T(128)S(1)}, s32[4]{0:T(128)}, u32[]{:S(2)}) copy-start(s32[4]{0:T(128)} %param.18) | copy-start | bytes 52
  0.8 0.7 %copy-start.11 = (s32[4]{0:T(128)S(1)}, s32[4]{0:T(128)}, u32[]{:S(2)}) copy-start(s32[4]{0:T(128)} %param.17) | copy-start | bytes 52
  2.5 0.9 %copy-start.9 = (s32[20736]{0:T(1024)S(1)}, s32[20736]{0:T(1024)}, u32[]{:S(2)}) copy-start(s32[20736]{0:T(1024)} %param.20) | copy-start | bytes 248836
  3.9 0.9 %copy-start.7 = (bf16[2,12,12,192]{3,0,2,1:T(2,128)(2,1)S(1)}, bf16[2,12,12,192]{3,0,2,1:T(2,128)(2,1)}, u32[]{:S(2)}) copy-start(bf16[2,12,12,192]{3,0,2,1:T(2,128)(2,1)} %param.11) | copy-start | bytes 331780
  4.8 0.9 %copy-start.8 = (bf16[2,12,12,192]{3,0,2,1:T(2,128)(2,1)S(1)}, bf16[2,12,12,192]{3,0,2,1:T(2,128)(2,1)}, u32[]{:S(2)}) copy-start(bf16[2,12,12,192]{3,0,2,1:T(2,128)(2,1)} %param.12) | copy-start | bytes 331780
  15.1 0.9 %copy-start.5 = (f32[12,144,128]{2,1,0:T(8,128)}, f32[12,144,128]{2,1,0:T(8,128)S(1)}, u32[]{:S(2)}) copy-start(f32[12,144,128]{2,1,0:T(8,128)S(1)} %get-tuple-element.17.bias_ref) | copy-start | bytes 2654212
  16.0 0.9 %copy-start.4 = (s32[192,192]{1,0:T(8,128)S(1)}, s32[192,192]{1,0:T(8,128)}, u32[]{:S(2)}) copy-start(s32[192,192]{1,0:T(8,128)} %proj_ref.1) | copy-start | bytes 442372
  16.1 1.1 %copy-start.2 = (s32[768,192]{0,1:T(8,128)S(1)}, s32[768,192]{0,1:T(8,128)}, u32[]{:S(2)}) copy-start(s32[768,192]{0,1:T(8,128)} %param.16) | copy-start | bytes 1769476
  16.2 1.2 %copy-start.1 = (s32[192,768]{1,0:T(8,128)S(1)}, s32[192,768]{1,0:T(8,128)}, u32[]{:S(2)}) copy-start(s32[192,768]{1,0:T(8,128)} %up_ref.1) | copy-start | bytes 1769476
  16.3 1.3 %copy-start.3 = (s32[192,576]{1,0:T(8,128)S(1)}, s32[192,576]{1,0:T(8,128)}, u32[]{:S(2)}) copy-start(s32[192,576]{1,0:T(8,128)} %qkv_ref.1) | copy-start | bytes 1327108
  17.6 1.2 %copy-start.6 = (f32[12,144,128]{2,1,0:T(8,128)S(1)}, f32[12,144,128]{2,1,0:T(8,128)}, u32[]{:S(2)}) copy-start(f32[12,144,128]{2,1,0:T(8,128)} %copy-done.5) | copy-start | bytes 2654212
